TPU v7x, 512 devices: a whole 4x4x16 slice. The times are simulated.
512 devices in a mesh: row: 16 (over z), col: 32 (over x, y, core).
Axes of the slice: x: 4, y: 4, z: 16, core: 2. Of those that a mesh axis runs over, the one named last changes fastest.
Arguments:
- kernel: float32 [2, 4096, 1, 8192], P(None, 'row', None, 'col'), may hold values from 0 to 2.5, as said below
Outputs:
- factored: float32 [2, 4096, 1, 8192], P(None, 'row', None, 'col')
Inputs may be any that keep to these rules, and one draw needn't show every extreme that they name: kernel holds a symmetric positive definite matrix of order 8192.
All inputs are finite; a program needn't handle non-finite values.
Results may differ from a plain program's by a relative error of at most 0.0003.
Values sent between devices are 32-bit elements; how exact they have to be, the bound alone decides.
No kernel may reach another device: no remote copies, remote signals or barrier semaphores. Data moves between devices by JAX's collectives and lax.ppermute only.
A program may use at most 64 MiB of HBM per device.

v0:
```python
import jax
import jax.numpy as jnp
from jax import lax
from jax.sharding import PartitionSpec as P

KP = 4


def spread(value, axis, source):
    kept = jnp.where(lax.axis_index(axis) == source, value, 0).astype(value.dtype)
    return lax.psum(kept, axis)


def solve_stack(factor, blocks):
    block_count, panel_width, _ = blocks.shape
    flat = blocks.reshape(block_count * panel_width, panel_width)
    solved = jax.scipy.linalg.solve_triangular(factor, flat.T, lower=True).T
    return solved.reshape(block_count, panel_width, panel_width)


def trailing(rows_panel, cols_panel):
    return jnp.einsum("lae,mbe->lamb", rows_panel, cols_panel, precision=lax.Precision.HIGHEST)


def on_device(kernel):
    row_blocks, panel_width, col_blocks, _ = kernel.shape
    grid_rows = lax.axis_size("row")
    grid_cols = lax.axis_size("col")
    col_ratio = grid_cols // grid_rows
    row_index = lax.axis_index("row")
    col_index = lax.axis_index("col")
    global_rows = jnp.arange(row_blocks, dtype=jnp.int32) * grid_rows + row_index
    global_cols = jnp.arange(col_blocks, dtype=jnp.int32) * grid_cols + col_index
    identity = jnp.eye(panel_width, dtype=jnp.float32)
    matrix = kernel
    for panel in range(KP):
        home_row = panel % grid_rows
        local_row = panel // grid_rows
        home_col = panel % grid_cols
        local_col = panel // grid_cols
        column = matrix[:, :, local_col, :]
        under_diag = (global_rows > panel)[:, None, None]
        at_column = col_index == home_col
        at_diagonal = jnp.logical_and(row_index == home_row, at_column)
        own_block = jnp.where(at_diagonal, column[local_row], identity)
        factor = spread(jnp.linalg.cholesky(own_block), "row", home_row)
        panel_here = jnp.where(under_diag, solve_stack(factor, column), 0.0)
        rows_panel = spread(panel_here, "col", home_col)
        grouped = rows_panel.reshape(col_blocks, col_ratio, panel_width, panel_width)
        chosen = lax.dynamic_index_in_dim(grouped, col_index // grid_rows, axis=1, keepdims=False)
        cols_panel = spread(chosen, "row", col_index % grid_rows)
        matrix = matrix - trailing(rows_panel, cols_panel)
        on_diagonal = (global_rows == panel)[:, None, None]
        new_column = jnp.where(under_diag, panel_here, jnp.where(on_diagonal, factor[None], 0.0))
        matrix = matrix.at[:, :, local_col, :].set(
            jnp.where(at_column, new_column, matrix[:, :, local_col, :])
        )
    upper_right = jnp.logical_and(
        (global_rows < KP)[:, None, None, None], (global_cols >= KP)[None, None, :, None]
    )
    return jnp.where(upper_right, 0.0, matrix)


def solution(mesh):
    in_specs = (P(None, "row", None, "col"),)
    out_specs = P(None, "row", None, "col")
    return jax.shard_map(
        on_device, mesh=mesh, in_specs=in_specs, out_specs=out_specs, check_vma=False
    )
```

profile of v0, /device:TPU:6, one launch (start us, length us, event | category | flops | bytes accessed | tf_op | source)
XLA Modules:
  0.0 1893.5 jit_solution(10594121639331819096)
XLA Ops:
  6.5 0.9 slice-done
  7.9 11.7 cholesky.214
  19.6 9.8 custom-call.17
  30.0 11.7 cholesky.231
  41.7 0.7 compare_reduce_fusion.6
  43.8 0.7 fusion.31
  45.1 139.5 %all-reduce.14.cloned.1.call-done = f32[256,256]{1,0:T(8,128)} async-done(((f32[256,256]{1,0:T(8,128)}), f32[256,256]{1,0:T(8,128)}) %all-reduce.14.cloned.1.call-update) | async-done | bytes 262160 | tf_op jit(solution)/shard_map/psum | solution.py:11
  184.6 1.0 fusion.21
  185.7 3.8 while.12
  186.3 1.3 bitcast_dynamic-update-slice_fusion.8
  188.2 1.3 bitcast_dynamic-update-slice_fusion.8
  189.5 19.7 %custom-call.18 = f32[2,128,128]{1,2,0:T(8,128)S(1)} custom-call(f32[2,128,128]{2,1,0:T(8,128)S(1)} %get-tuple-element.81), custom_call_target="InvertDiagBlocksLowerTriangular" | custom-call | tf_op jit(solution)/shard_map/jit(_solve_triangular)/triangular_solve | solution.py:17
  211.1 0.9 select_select_fusion.5
  212.1 132.0 %all-reduce.16.cloned.1.call-done = f32[2,256,256]{1,2,0:T(8,128)} async-done(((f32[2,256,256]{1,2,0:T(8,128)}), f32[2,256,256]{1,2,0:T(8,128)}) %all-reduce.16.cloned.1.call-update) | async-done | bytes 524304 | tf_op jit(solution)/shard_map/psum | solution.py:11
  344.1 1.7 select_bitcast_fusion.6
  347.0 0.8 copy.29
  347.8 132.9 %all-reduce.18.cloned.1.call-done = f32[256,256]{0,1:T(8,128)} async-done(((f32[256,256]{0,1:T(8,128)}), f32[256,256]{0,1:T(8,128)}) %all-reduce.18.cloned.1.call-update) | async-done | bytes 262160 | tf_op jit(solution)/shard_map/psum | solution.py:11
  480.7 1.9 bitcast_select_fusion
  482.9 11.7 cholesky.248
  494.6 9.8 custom-call.19
  504.9 11.7 cholesky.265
  519.4 0.7 fusion.30
  521.0 131.6 %all-reduce.20.cloned.1.call-done = f32[256,256]{1,0:T(8,128)} async-done(((f32[256,256]{1,0:T(8,128)}), f32[256,256]{1,0:T(8,128)}) %all-reduce.20.cloned.1.call-update) | async-done | bytes 262160 | tf_op jit(solution)/shard_map/psum | solution.py:11
  652.6 1.0 fusion.23
  653.5 4.1 while.13
  654.2 1.4 bitcast_dynamic-update-slice_fusion.9
  656.2 1.4 bitcast_dynamic-update-slice_fusion.9
  657.7 19.7 %custom-call.20 = f32[2,128,128]{1,2,0:T(8,128)S(1)} custom-call(f32[2,128,128]{2,1,0:T(8,128)S(1)} %get-tuple-element.82), custom_call_target="InvertDiagBlocksLowerTriangular" | custom-call | tf_op jit(solution)/shard_map/jit(_solve_triangular)/triangular_solve | solution.py:17
  679.0 0.9 select_select_fusion.4
  680.0 132.0 %all-reduce.22.cloned.1.call-done = f32[2,256,256]{1,2,0:T(8,128)} async-done(((f32[2,256,256]{1,2,0:T(8,128)}), f32[2,256,256]{1,2,0:T(8,128)}) %all-reduce.22.cloned.1.call-update) | async-done | bytes 524304 | tf_op jit(solution)/shard_map/psum | solution.py:11
  812.0 1.7 select_bitcast_fusion.5
  815.0 133.6 %all-reduce.24.cloned.1.call-done = f32[256,256]{0,1:T(8,128)} async-done(((f32[256,256]{0,1:T(8,128)}), f32[256,256]{0,1:T(8,128)}) %all-reduce.24.cloned.1.call-update) | async-done | bytes 262160 | tf_op jit(solution)/shard_map/psum | solution.py:11
  948.6 1.8 select_select_fusion.1
  950.7 11.7 cholesky.282
  962.5 9.8 custom-call.21
  972.8 11.7 cholesky.299
  987.0 0.7 fusion.29
  988.8 131.3 %all-reduce.26.cloned.1.call-done = f32[256,256]{1,0:T(8,128)} async-done(((f32[256,256]{1,0:T(8,128)}), f32[256,256]{1,0:T(8,128)}) %all-reduce.26.cloned.1.call-update) | async-done | bytes 262160 | tf_op jit(solution)/shard_map/psum | solution.py:11
  1120.2 1.0 fusion.25
  1121.1 3.8 while.14
  1121.8 1.3 bitcast_dynamic-update-slice_fusion.10
  1123.7 1.3 bitcast_dynamic-update-slice_fusion.10
  1125.0 19.7 %custom-call.22 = f32[2,128,128]{1,2,0:T(8,128)S(1)} custom-call(f32[2,128,128]{2,1,0:T(8,128)S(1)} %get-tuple-element.83), custom_call_target="InvertDiagBlocksLowerTriangular" | custom-call | tf_op jit(solution)/shard_map/jit(_solve_triangular)/triangular_solve | solution.py:17
  1146.3 0.9 select_select_fusion.3
  1147.3 132.0 %all-reduce.28.cloned.1.call-done = f32[2,256,256]{1,2,0:T(8,128)} async-done(((f32[2,256,256]{1,2,0:T(8,128)}), f32[2,256,256]{1,2,0:T(8,128)}) %all-reduce.28.cloned.1.call-update) | async-done | bytes 524304 | tf_op jit(solution)/shard_map/psum | solution.py:11
  1279.4 1.7 select_bitcast_fusion.4
  1282.4 133.7 %all-reduce.30.cloned.1.call-done = f32[256,256]{0,1:T(8,128)} async-done(((f32[256,256]{0,1:T(8,128)}), f32[256,256]{0,1:T(8,128)}) %all-reduce.30.cloned.1.call-update) | async-done | bytes 262160 | tf_op jit(solution)/shard_map/psum | solution.py:11
  1416.0 1.8 select_select_fusion
  1418.1 11.7 cholesky.316
  1429.9 9.8 custom-call.23
  1440.2 11.7 cholesky.333
  1454.6 0.7 fusion.28
  1456.2 131.6 %all-reduce.32.cloned.1.call-done = f32[256,256]{1,0:T(8,128)} async-done(((f32[256,256]{1,0:T(8,128)}), f32[256,256]{1,0:T(8,128)}) %all-reduce.32.cloned.1.call-update) | async-done | bytes 262160 | tf_op jit(solution)/shard_map/psum | solution.py:11
  1587.7 1.0 fusion.27
  1588.7 4.1 while.15
  1589.4 1.4 bitcast_dynamic-update-slice_fusion.11
  1591.4 1.4 bitcast_dynamic-update-slice_fusion.11
  1592.9 19.7 %custom-call.24 = f32[2,128,128]{1,2,0:T(8,128)S(1)} custom-call(f32[2,128,128]{2,1,0:T(8,128)S(1)} %get-tuple-element.84), custom_call_target="InvertDiagBlocksLowerTriangular" | custom-call | tf_op jit(solution)/shard_map/jit(_solve_triangular)/triangular_solve | solution.py:17
  1614.2 0.9 select_select_fusion.2
  1615.2 132.0 %all-reduce.34.cloned.1.call-done = f32[2,256,256]{1,2,0:T(8,128)} async-done(((f32[2,256,256]{1,2,0:T(8,128)}), f32[2,256,256]{1,2,0:T(8,128)}) %all-reduce.34.cloned.1.call-update) | async-done | bytes 524304 | tf_op jit(solution)/shard_map/psum | solution.py:11
  1747.2 1.7 select_bitcast_fusion.3
  1749.1 134.7 %all-reduce.36.cloned.1.call-done = f32[256,256]{0,1:T(8,128)} async-done(((f32[256,256]{0,1:T(8,128)}), f32[256,256]{0,1:T(8,128)}) %all-reduce.36.cloned.1.call-update) | async-done | bytes 262160 | tf_op jit(solution)/shard_map/psum | solution.py:11
  1883.8 1.7 fusion.2
  1885.5 1.0 copy.67
  (167 shorter events, 26.2 us)
Async XLA Ops:
  6.5 178.1 %all-reduce.14.cloned.1.call-start = ((), (), s32[]{:S(2)}) async-start(), calls=%async_computation | async-start | bytes 524288 | tf_op jit(solution)/shard_map/psum | solution.py:11
  6.5 0.9 slice-start
  30.0 15.1 copy-start
  44.5 299.5 %all-reduce.16.cloned.1.call-start = ((), (), s32[]{:S(2)}) async-start(), calls=%async_computation.1 | async-start | bytes 1048576 | tf_op jit(solution)/shard_map/psum | solution.py:11
  212.0 268.7 %all-reduce.18.cloned.1.call-start = ((), (), s32[]{:S(2)}) async-start(), calls=%async_computation.2 | async-start | bytes 524288 | tf_op jit(solution)/shard_map/psum | solution.py:11
  345.8 1.0 copy-start.1
  345.8 306.8 %all-reduce.20.cloned.1.call-start = ((), (), s32[]{:S(2)}) async-start(), calls=%async_computation.3 | async-start | bytes 524288 | tf_op jit(solution)/shard_map/psum | solution.py:11
  520.1 291.9 %all-reduce.22.cloned.1.call-start = ((), (), s32[]{:S(2)}) async-start(), calls=%async_computation.4 | async-start | bytes 1048576 | tf_op jit(solution)/shard_map/psum | solution.py:11
  680.0 268.7 %all-reduce.24.cloned.1.call-start = ((), (), s32[]{:S(2)}) async-start(), calls=%async_computation.5 | async-start | bytes 524288 | tf_op jit(solution)/shard_map/psum | solution.py:11
  813.7 0.9 copy-start.2
  813.7 306.4 %all-reduce.26.cloned.1.call-start = ((), (), s32[]{:S(2)}) async-start(), calls=%async_computation.6 | async-start | bytes 524288 | tf_op jit(solution)/shard_map/psum | solution.py:11
  987.8 291.6 %all-reduce.28.cloned.1.call-start = ((), (), s32[]{:S(2)}) async-start(), calls=%async_computation.7 | async-start | bytes 1048576 | tf_op jit(solution)/shard_map/psum | solution.py:11
  1147.3 268.7 %all-reduce.30.cloned.1.call-start = ((), (), s32[]{:S(2)}) async-start(), calls=%async_computation.8 | async-start | bytes 524288 | tf_op jit(solution)/shard_map/psum | solution.py:11
  1281.0 0.9 copy-start.3
  1281.1 306.7 %all-reduce.32.cloned.1.call-start = ((), (), s32[]{:S(2)}) async-start(), calls=%async_computation.9 | async-start | bytes 524288 | tf_op jit(solution)/shard_map/psum | solution.py:11
  1455.4 291.8 %all-reduce.34.cloned.1.call-start = ((), (), s32[]{:S(2)}) async-start(), calls=%async_computation.10 | async-start | bytes 1048576 | tf_op jit(solution)/shard_map/psum | solution.py:11
  1615.2 268.6 %all-reduce.36.cloned.1.call-start = ((), (), s32[]{:S(2)}) async-start(), calls=%async_computation.11 | async-start | bytes 524288 | tf_op jit(solution)/shard_map/psum | solution.py:11
  1747.2 1.8 copy-start.5
  1748.9 134.9 %copy-start.4 = (f32[2,256,256]{1,2,0:T(8,128)S(1)}, f32[2,256,256]{1,2,0:T(8,128)}, u32[]{:S(2)}) copy-start(f32[2,256,256]{1,2,0:T(8,128)} %all-reduce.34.cloned.1.call-done) | copy-start | bytes 1572868
Sparse Core Ops, SparseCore 0:
  44.7 139.9 all-reduce.13
  212.1 131.8 all-reduce.15
  346.4 134.2 all-reduce.17
  520.3 132.2 all-reduce.19
  680.1 131.8 all-reduce.21
  814.3 134.3 all-reduce.23
  987.9 132.2 all-reduce.25
  1147.4 131.9 all-reduce.27
  1281.7 134.2 all-reduce.29
  1455.5 132.2 all-reduce.31
  1615.3 131.8 all-reduce.33
  1749.4 134.3 all-reduce.35
where the time goes:
time: 1900 us; the launch traced here: 1890 us
  waiting for transfers between devices  1600 us (84%)
  other arithmetic  235 us (12%)
  local copies, waits for them, and re-layouts  25.8 us (1%)
  between operations  19.8 us (1%)
    psum x12, waiting for transfers between devices, spread(): return lax.psum(kept, axis)  1600 us
    another operation x27, other arithmetic, on_device(): factor = spread(jnp.linalg.cholesky(own_block), 'row', home_row)  138 us
    another operation x9, other arithmetic, solve_stack(): solved = jax.scipy.linalg.solve_triangular(factor, flat.T, lower=True).T  82.6 us
  transfers between devices with their start and end apart: 12, of which 12 were waited for; matrix products, arithmetic and copies ran while one was open for 0% of the time, Pallas kernels for 0%

commit v1 on v0

v1 whole, which is shorter than its diff:
```python
import jax
import jax.numpy as jnp
from jax import lax
from jax.experimental import pallas as pl
from jax.experimental.pallas import tpu as pltpu
from jax.sharding import PartitionSpec as P

KP = 4
NB = 256
F32 = jnp.float32
VMEM_LIMIT = 48 * 1024 * 1024


def _dot(a, b, dims):
    return lax.dot_general(
        a, b, (dims, ((), ())), precision=lax.Precision.HIGHEST, preferred_element_type=F32
    )


def _nn(a, b):
    return _dot(a, b, ((1,), (0,)))


def _nt(a, b):
    return _dot(a, b, ((1,), (1,)))


def _tn(a, b):
    return _dot(a, b, ((0,), (0,)))


def _factor_tile(tile):
    count = tile.shape[0] // 8
    rows = [tile[8 * s : 8 * s + 8] for s in range(count)]
    lane = lax.broadcasted_iota(jnp.int32, (8, 128), 1)
    sub = lax.broadcasted_iota(jnp.int32, (8, 128), 0)

    def spread(x):
        return jnp.broadcast_to(x, (8, 128))

    upper, inverse = [], []
    for s in range(count):
        base = 8 * s
        here = (lane >= base) & (lane < base + 8)
        cols = {t: [spread(rows[t][:, base + k : base + k + 1]) for k in range(8)] for t in range(s, count)}
        rows[s] = jnp.where(here, jnp.where(lane - base == sub, 1.0, 0.0), rows[s])
        for t in range(s + 1, count):
            rows[t] = jnp.where(here, 0.0, rows[t])
        own = cols[s]
        scales, pivots, pivot_rows = [], {}, []
        for j in range(8):
            scale = 1.0 / spread(own[j][j : j + 1, :])
            ratio = jnp.where(sub > j, own[j] * scale, 0.0)
            pivot_row = spread(rows[s][j : j + 1, :])
            for k in range(j + 1, 8):
                pivots[j, k] = spread(own[k][j : j + 1, :])
                own[k] = own[k] - ratio * pivots[j, k]
            rows[s] = rows[s] - ratio * pivot_row
            scales.append(scale)
            pivot_rows.append(pivot_row)
        for t in range(s + 1, count):
            other, row = cols[t], rows[t]
            for j in range(8):
                ratio = other[j] * scales[j]
                for k in range(j + 1, 8):
                    other[k] = other[k] - ratio * pivots[j, k]
                row = row - ratio * pivot_rows[j]
            rows[t] = row
        diag, square = own[0], own[0]
        for k in range(1, 8):
            diag = jnp.where(sub == k, own[k], diag)
            square = jnp.where(lane == base + k, own[k], square)
        root = lax.rsqrt(diag)
        square = jnp.where(sub <= lane - base, square, 0.0)
        upper.append(jnp.where(lane < base, 0.0, jnp.where(here, square, rows[s])) * root)
        inverse.append(jnp.where(lane < base + 8, rows[s], 0.0) * root)
    return jnp.concatenate(upper, 0), jnp.concatenate(inverse, 0)


def _factor_block(block):
    h = NB // 2
    u11, v11 = _factor_tile(block[:h, :h])
    u12 = _nn(v11, block[:h, h:])
    u22, v22 = _factor_tile(block[h:, h:] - _tn(u12, u12))
    v21 = -_nn(v22, _tn(u12, v11))
    zero = jnp.zeros((h, h), F32)
    upper = jnp.concatenate([jnp.concatenate([u11, u12], 1), jnp.concatenate([zero, u22], 1)], 0)
    inverse = jnp.concatenate([jnp.concatenate([v11, zero], 1), jnp.concatenate([v21, v22], 1)], 0)
    return upper, inverse


UPPER = [(i, j) for i in range(KP) for j in range(i, KP)]


def _factor_kernel(pieces, upper, inverse, work):
    for slot, (i, j) in enumerate(UPPER):
        work[i, j] = pieces[:, slot].reshape(NB, NB)

    def panel(k, _):
        u, v = _factor_block(work[k, k])
        upper[k, k] = u
        inverse[k] = v

        def solve(j, _):
            upper[k, j] = _nn(inverse[k], work[k, j])
            return 0

        lax.fori_loop(k + 1, KP, solve, 0)

        def down(i, _):
            def across(j, _):
                work[i, j] = work[i, j] - _tn(upper[k, i], upper[k, j])
                return 0

            return lax.fori_loop(i, KP, across, 0)

        lax.fori_loop(k + 1, KP, down, 0)
        return 0

    lax.fori_loop(0, KP, panel, 0)


def _finish_kernel(where, kernel, left, top, upper, inverse, out, left_rows, top_cols):
    row, col = where[0], where[1]
    for k in range(KP):
        part = jnp.concatenate([left[:, k, l].reshape(NB, NB) for l in range(2)], 0)
        head = top[k]
        for j in range(k):
            part = part - _nn(left_rows[j], upper[j, k])
            head = head - _tn(upper[j, k], top_cols[j])
        left_rows[k] = _nt(part, inverse[k])
        top_cols[k] = _nn(inverse[k], head)

    @pl.when(col >= KP)
    def _():
        total = kernel[...].reshape(2 * NB, NB)
        for k in range(KP):
            total = total - _nn(left_rows[k], top_cols[k])
        total = total.reshape(2, NB, NB)
        out[0] = jnp.where(row < KP, 0.0, total[0])
        out[1] = total[1]

    @pl.when(col < KP)
    def _():
        block = left_rows[col].reshape(2, NB, NB)
        out[0] = jnp.where(row < col, 0.0, block[0])
        out[1] = block[1]

    @pl.when((row == col) & (col < KP))
    def _():
        out[0] = upper[col, col].T


def on_device(kernel):
    rows_axis, cols_axis = lax.axis_size("row"), lax.axis_size("col")
    row_index, col_index = lax.axis_index("row"), lax.axis_index("col")
    blocks = kernel.reshape(2, NB, NB)
    thin = NB // cols_axis

    top = lax.all_gather(blocks[0], "row")[:KP]

    cut = blocks.reshape(2, cols_axis, thin, NB).swapaxes(0, 1)
    scattered = lax.all_to_all(cut, "col", 0, 0)[:KP]

    corner = lax.all_to_all(
        jnp.broadcast_to(scattered[:, 0][None], (rows_axis, KP, thin, NB)), "row", 0, 0
    )[:KP]
    corner = jnp.stack([corner[i, j] for i, j in UPPER])
    pieces = lax.all_to_all(
        jnp.broadcast_to(corner[None], (cols_axis, len(UPPER), thin, NB)), "col", 0, 0
    )
    left = lax.all_to_all(
        jnp.broadcast_to(scattered[None], (cols_axis, KP, 2, thin, NB)), "col", 0, 0
    )
    vmem = pl.BlockSpec(memory_space=pltpu.VMEM)
    params = pltpu.CompilerParams(vmem_limit_bytes=VMEM_LIMIT)
    upper, inverse = pl.pallas_call(
        _factor_kernel,
        out_shape=(
            jax.ShapeDtypeStruct((KP, KP, NB, NB), F32),
            jax.ShapeDtypeStruct((KP, NB, NB), F32),
        ),
        in_specs=[vmem],
        out_specs=(vmem, vmem),
        scratch_shapes=[pltpu.VMEM((KP, KP, NB, NB), F32)],
        compiler_params=params,
        cost_estimate=pl.CostEstimate(flops=50_000_000_000, bytes_accessed=8_000_000, transcendentals=0),
        name="factor",
    )(pieces)
    place = jnp.stack([row_index, col_index]).astype(jnp.int32)
    out = pl.pallas_call(
        _finish_kernel,
        out_shape=jax.ShapeDtypeStruct((2, NB, NB), F32),
        in_specs=[pl.BlockSpec(memory_space=pltpu.SMEM)] + [vmem] * 5,
        out_specs=vmem,
        scratch_shapes=[pltpu.VMEM((KP, 2 * NB, NB), F32), pltpu.VMEM((KP, NB, NB), F32)],
        compiler_params=params,
        cost_estimate=pl.CostEstimate(flops=10_000_000_000, bytes_accessed=8_000_000, transcendentals=0),
        name="finish",
    )(place, blocks, left, top, upper, inverse)
    return out.reshape(kernel.shape)


def solution(mesh):
    spec = P(None, "row", None, "col")
    return jax.shard_map(
        on_device, mesh=mesh, in_specs=(spec,), out_specs=spec, check_vma=False
    )
```

time: 1900 us -> 190 us (0.10)
  waiting for transfers between devices: 1600 us -> 60.1 us
  other arithmetic: 235 us -> 0.08 us
  Pallas kernels: 0 us -> 56.1 us
  starting transfers between devices: 1.68 us -> 29.4 us
    psum x12 -> x0, waiting for transfers between devices: 1600 us -> none  [spread(): return lax.psum(kept, axis)]
    another operation x40 -> x1, other arithmetic: 227 us -> 0.08 us  [on_device(): place = jnp.stack([row_index, col_index]).astype(jnp.int32)]
    all_to_all x0 -> x3, waiting for transfers between devices: none -> 60.1 us  [the longest x1 31.7 us: on_device(): lax.all_to_all(jnp.broadcast_to(corner[None], (cols_axis, len(UPPER), thi...]
    pallas_call x0 -> x2, Pallas kernels: none -> 56.1 us  [the longest x1 43.9 us: on_device(): pl.pallas_call(_factor_kernel, out_shape=(jax.ShapeDtypeStruct((KP, KP, N...]
    all_to_all x0 -> x3, starting transfers between devices: none -> 29.4 us  [the longest x1 13.9 us: on_device(): lax.all_to_all(jnp.broadcast_to(scattered[:, 0][None], (rows_axis, KP, th...]
  transfers between devices with their start and end apart: 12 -> 4, of which waited for: 12 -> 2; matrix products, arithmetic and copies ran while one was open for 0% -> 3% of each run, Pallas kernels for 0% -> 23%
where the time goes in v1:
time: 190 us; the launch traced here: 189 us
  waiting for transfers between devices  60.1 us (32%)
  Pallas kernels  56.1 us (30%)
  starting transfers between devices  29.4 us (15%)
  blocking collectives  18 us (9%)
  between operations  13.5 us (7%)
  local copies, waits for them, and re-layouts  11.9 us (6%)
    pallas_call x1, Pallas kernels, on_device(): pl.pallas_call(_factor_kernel, out_shape=(jax.ShapeDtypeStruct((KP, KP, N...  43.9 us
    all_to_all x1, waiting for transfers between devices, on_device(): lax.all_to_all(jnp.broadcast_to(corner[None], (cols_axis, len(UPPER), thi...  31.7 us
    all_to_all x1, waiting for transfers between devices, on_device(): lax.all_to_all(jnp.broadcast_to(scattered[:, 0][None], (rows_axis, KP, th...  28.4 us
    all_to_all x1, blocking collectives, on_device(): scattered = lax.all_to_all(cut, 'col', 0, 0)[:KP]  18 us
    all_to_all x1, starting transfers between devices, on_device(): lax.all_to_all(jnp.broadcast_to(scattered[:, 0][None], (rows_axis, KP, th...  13.9 us
    pallas_call x1, Pallas kernels, on_device(): pl.pallas_call(_finish_kernel, out_shape=jax.ShapeDtypeStruct((2, NB, NB)...  12.2 us
    all_to_all x1, starting transfers between devices, on_device(): lax.all_to_all(jnp.broadcast_to(corner[None], (cols_axis, len(UPPER), thi...  7.88 us
    all_to_all x1, starting transfers between devices, on_device(): lax.all_to_all(jnp.broadcast_to(scattered[None], (cols_axis, KP, 2, thin,...  7.56 us
  transfers between devices with their start and end apart: 4, of which 2 were waited for; matrix products, arithmetic and copies ran while one was open for 3% of the time, Pallas kernels for 23%

profile of v1, /device:TPU:6, one launch (start us, length us, event | category | flops | bytes accessed | tf_op | source)
XLA Modules:
  0.0 189.1 jit_solution(4058432810939912075)
XLA Ops:
  6.5 0.0 slice-start
  6.5 1.1 copy.16
  7.7 0.1 copy.15
  7.7 18.0 %all_to_all.20 = f32[32,2,8,256]{3,2,1,0:T(8,128)S(1)} all-to-all(f32[32,2,8,256]{3,2,1,0:T(8,128)S(1)} %bitcast.59), channel_id=1, replica_groups=mesh['row'=16,'col'=32] {'col'}, dimensions={0} | all-to-all | bytes 1048576 | tf_op jit(solution)/shard_map/all_to_all | solution.py:163
  25.7 0.0 copy-start.2
  25.7 0.8 copy-done.2
  26.5 0.9 broadcast_in_dim.10
  27.4 13.9 %all-to-all-start.2 = ((f32[16,4,8,256]{3,2,1,0:T(8,128)}), f32[16,4,8,256]{3,2,1,0:T(8,128)S(1)}, u32[]{:S(2)}, u32[]{:S(2)}) async-start(f32[16,4,8,256]{3,2,1,0:T(8,128)} %broadcast_in_dim.10), calls=%async_computation.2 | async-start | bytes 1048576 | tf_op jit(solution)/shard_map/all_to_all | solution.py:165
  41.3 0.0 all-gather.3.cloned.1.call-start
  41.3 0.0 slice-done
  41.4 0.7 copy.11
  42.1 0.0 all-gather.3.cloned.1.call-update
  42.1 28.4 %all-to-all-done.2 = f32[16,4,8,256]{3,2,1,0:T(8,128)S(1)} async-done(((f32[16,4,8,256]{3,2,1,0:T(8,128)}), f32[16,4,8,256]{3,2,1,0:T(8,128)S(1)}, u32[]{:S(2)}, u32[]{:S(2)}) %all-to-all-start.2) | async-done | bytes 524320 | tf_op jit(solution)/shard_map/all_to_all | solution.py:165
  70.6 1.8 broadcast_in_dim.22
  72.4 0.0 slice-start.1
  72.4 7.9 %all-to-all-start.3 = ((f32[32,10,8,256]{3,2,1,0:T(8,128)}), f32[32,10,8,256]{3,2,1,0:T(8,128)S(1)}, u32[]{:S(2)}, u32[]{:S(2)}) async-start(f32[32,10,8,256]{3,2,1,0:T(8,128)} %broadcast_in_dim.22), calls=%async_computation.3 | async-start | bytes 5242880 | tf_op jit(solution)/shard_map/all_to_all | solution.py:169
  80.3 0.1 pad_add_fusion.where
  80.4 31.7 %all-to-all-done.3.pieces = f32[32,10,8,256]{3,2,1,0:T(8,128)S(1)} async-done(((f32[32,10,8,256]{3,2,1,0:T(8,128)}), f32[32,10,8,256]{3,2,1,0:T(8,128)S(1)}, u32[]{:S(2)}, u32[]{:S(2)}) %all-to-all-start.3) | async-done | bytes 2621472 | tf_op jit(solution)/shard_map/all_to_all | solution.py:169
  112.1 0.0 slice-done.1
  112.1 1.6 broadcast_in_dim.8
  113.7 7.6 %all-to-all-start.1 = ((f32[32,4,2,8,256]{4,3,2,1,0:T(8,128)}), f32[32,4,2,8,256]{4,3,2,1,0:T(8,128)}, u32[]{:S(2)}, u32[]{:S(2)}) async-start(f32[32,4,2,8,256]{4,3,2,1,0:T(8,128)} %broadcast_in_dim.8), calls=%async_computation.1 | async-start | bytes 4194304 | tf_op jit(solution)/shard_map/all_to_all | solution.py:172
  121.2 43.9 %factor.1 = (f32[4,4,256,256]{3,2,1,0:T(8,128)}, f32[4,256,256]{2,1,0:T(8,128)S(1)}) custom-call(f32[32,10,8,256]{3,2,1,0:T(8,128)S(1)} %all-to-all-done.3.pieces), custom_call_target="tpu_custom_call" | custom-call | flops 49999998976 | bytes 8000000 | tf_op jit(solution)/shard_map/factor/pallas_call | solution.py:177
  165.1 0.0 copy-start
  165.1 1.0 copy-done
  166.1 0.0 all-gather.3.cloned.1.call-done
  166.1 1.3 slice_bitcast_fusion.top
  167.4 0.0 all-to-all-done.1.left
  167.4 0.0 copy-start.1
  167.4 1.2 copy-done.1
  168.7 12.2 %finish.1 = f32[2,256,256]{2,1,0:T(8,128)S(1)} custom-call(s32[2]{0:T(128)S(1)} %pad_add_fusion.where, f32[2,256,256]{2,1,0:T(8,128)S(1)} %bitcast.57, f32[32,4,2,8,256]{4,3,2,1,0:T(8,128)} %all-to-all-done.1.left, f32[4,256,256]{2,1,0:T(8,128)S(1)} %slice_bitcast_fusion.top, f32[4,4,256,256]{3,2,1,0:T(8,128)} %get-tuple-element.7.upper, ...), custom_call_target="tpu_custom_call" | custom-call | flops 10000000000 | bytes 8000000 | tf_op jit(solution)/shard_map/finish/pallas_call | solution.py:191
  180.9 1.3 copy.8
  (11 shorter events, 0.0 us)
Async XLA Ops:
  6.5 34.8 %slice-start = ((f32[2,256,1,256]{3,2,1,0:T(1,128)}), f32[1,256,1,256]{3,2,1,0:T(1,128)S(1)}, s32[]{:S(2)}) async-start(f32[2,256,1,256]{3,2,1,0:T(1,128)} %param.1), calls=%async_computation.5 | async-start | bytes 524288 | tf_op jit(solution)/shard_map/slice | solution.py:160
  25.7 0.8 copy-start.2
  27.4 43.1 %all-to-all-start.2 = ((f32[16,4,8,256]{3,2,1,0:T(8,128)}), f32[16,4,8,256]{3,2,1,0:T(8,128)S(1)}, u32[]{:S(2)}, u32[]{:S(2)}) async-start(f32[16,4,8,256]{3,2,1,0:T(8,128)} %broadcast_in_dim.10), calls=%async_computation.2 | async-start | bytes 1048576 | tf_op jit(solution)/shard_map/all_to_all | solution.py:165
  41.3 124.8 %all-gather.3.cloned.1.call-start = ((), (), s32[]{:S(2)}) async-start(), calls=%async_computation.4 | async-start | bytes 4456448 | tf_op jit(solution)/shard_map/all_gather | solution.py:160
  72.4 39.7 %slice-start.1 = ((f32[32,2,8,256]{3,2,1,0:T(8,128)}), f32[4,2,8,256]{3,2,1,0:T(8,128)S(1)}, s32[]{:S(2)}) async-start(f32[32,2,8,256]{3,2,1,0:T(8,128)} %copy-done.2), calls=%async_computation.6 | async-start | bytes 131072 | tf_op jit(solution)/shard_map/slice | solution.py:163
  72.4 39.7 %all-to-all-start.3 = ((f32[32,10,8,256]{3,2,1,0:T(8,128)}), f32[32,10,8,256]{3,2,1,0:T(8,128)S(1)}, u32[]{:S(2)}, u32[]{:S(2)}) async-start(f32[32,10,8,256]{3,2,1,0:T(8,128)} %broadcast_in_dim.22), calls=%async_computation.3 | async-start | bytes 5242880 | tf_op jit(solution)/shard_map/all_to_all | solution.py:169
  113.7 53.8 %all-to-all-start.1 = ((f32[32,4,2,8,256]{4,3,2,1,0:T(8,128)}), f32[32,4,2,8,256]{4,3,2,1,0:T(8,128)}, u32[]{:S(2)}, u32[]{:S(2)}) async-start(f32[32,4,2,8,256]{4,3,2,1,0:T(8,128)} %broadcast_in_dim.8), calls=%async_computation.1 | async-start | bytes 4194304 | tf_op jit(solution)/shard_map/all_to_all | solution.py:172
  165.1 1.0 copy-start
  167.4 1.2 copy-start.1
Sparse Core Ops, SparseCore 0:
  44.2 81.9 all-gather.2

commit v2 on v1

v2 whole, which is shorter than its diff:
```python
import jax
import jax.numpy as jnp
from jax import lax
from jax.experimental import pallas as pl
from jax.experimental.pallas import tpu as pltpu
from jax.sharding import PartitionSpec as P

KP = 4
GROUP = 8
NB = 256
F32 = jnp.float32
MIB = 1024 * 1024


def _dot(a, b, dims):
    return lax.dot_general(
        a, b, (dims, ((), ())), precision=lax.Precision.HIGHEST, preferred_element_type=F32
    )


def _nn(a, b):
    return _dot(a, b, ((1,), (0,)))


def _nt(a, b):
    return _dot(a, b, ((1,), (1,)))


def _tn(a, b):
    return _dot(a, b, ((0,), (0,)))


def _factor_tile(tile):
    count = tile.shape[0] // 8
    rows = [tile[8 * s : 8 * s + 8] for s in range(count)]
    lane = lax.broadcasted_iota(jnp.int32, (8, 128), 1)
    sub = lax.broadcasted_iota(jnp.int32, (8, 128), 0)

    def spread(x):
        return jnp.broadcast_to(x, (8, 128))

    def column(x, at):
        return jnp.take_along_axis(x, jnp.full((8, 128), at, jnp.int32), axis=1)

    upper, inverse = [], []
    own = [column(rows[0], k) for k in range(8)]
    for s in range(count):
        base = 8 * s
        stop = (s // GROUP + 1) * GROUP
        last = s + 1 == stop
        here = (lane >= base) & (lane < base + 8)
        ahead = [] if last else [column(rows[s], base + 8 + k) for k in range(8)]
        below = [] if last else [column(rows[s + 1], base + k) for k in range(8)]
        after = [] if last else [column(rows[s + 1], base + 8 + k) for k in range(8)]
        cols = {t: [column(rows[t], base + k) for k in range(8)] for t in range(s + 2, stop)}
        rows[s] = jnp.where(here, jnp.where(lane - base == sub, 1.0, 0.0), rows[s])
        for t in range(s + 1, stop):
            rows[t] = jnp.where(here, 0.0, rows[t])
        scales, pivots, pivot_rows = [], {}, []
        for j in range(8):
            scale = 1.0 / spread(own[j][j : j + 1, :])
            ratio = jnp.where(sub > j, own[j], 0.0) * scale
            for k in range(j + 1, 8):
                pivots[j, k] = spread(own[k][j : j + 1, :])
                own[k] = own[k] - ratio * pivots[j, k]
            pivot_row = spread(rows[s][j : j + 1, :])
            rows[s] = rows[s] - ratio * pivot_row
            scales.append(scale)
            pivot_rows.append(pivot_row)
            if not last:
                low = below[j] * scale
                for k in range(j + 1, 8):
                    below[k] = below[k] - low * pivots[j, k]
                for k in range(8):
                    pivot = spread(ahead[k][j : j + 1, :])
                    ahead[k] = ahead[k] - ratio * pivot
                    after[k] = after[k] - low * pivot
                rows[s + 1] = rows[s + 1] - low * pivot_row
        for t in range(s + 2, stop):
            other, row = cols[t], rows[t]
            for j in range(8):
                ratio = other[j] * scales[j]
                for k in range(j + 1, 8):
                    other[k] = other[k] - ratio * pivots[j, k]
                row = row - ratio * pivot_rows[j]
            rows[t] = row
        diag, square = own[0], own[0]
        for k in range(1, 8):
            diag = jnp.where(sub == k, own[k], diag)
            square = jnp.where(lane == base + k, own[k], square)
        root = lax.rsqrt(diag)
        square = jnp.where(sub <= lane - base, square, 0.0)
        upper.append(jnp.where(lane < base, 0.0, jnp.where(here, square, rows[s])) * root)
        inverse.append(jnp.where(lane < base + 8, rows[s], 0.0) * root)
        own = after
        if last and stop < count:
            low, high = 8 * (stop - GROUP), 8 * stop
            done = jnp.concatenate(upper[-GROUP:], 0)
            kept = jnp.where(lax.broadcasted_iota(jnp.int32, done.shape, 1) < high, jnp.concatenate(inverse[-GROUP:], 0), done)
            change = _tn(done, kept)
            for t in range(stop, count):
                inside = (lane >= low) & (lane < high)
                rows[t] = jnp.where(inside, 0.0, rows[t]) - change[8 * t : 8 * t + 8]
            own = [column(rows[stop], 8 * stop + k) for k in range(8)]
    return jnp.concatenate(upper, 0), jnp.concatenate(inverse, 0)


def _factor_block(block):
    h = NB // 2
    u11, v11 = _factor_tile(block[:h, :h])
    u12 = _nn(v11, block[:h, h:])
    u22, v22 = _factor_tile(block[h:, h:] - _tn(u12, u12))
    v21 = -_nn(v22, _tn(u12, v11))
    zero = jnp.zeros((h, h), F32)
    upper = jnp.concatenate([jnp.concatenate([u11, u12], 1), jnp.concatenate([zero, u22], 1)], 0)
    inverse = jnp.concatenate([jnp.concatenate([v11, zero], 1), jnp.concatenate([v21, v22], 1)], 0)
    return upper, inverse


EARLY = [(0, 0), (0, 1), (1, 1)]
LATE = [(1, 2), (2, 2), (2, 3), (3, 3), (3, 0), (0, 2), (1, 3)]


def _fetch(pairs, sems):
    copies = [pltpu.make_async_copy(x, y, sems.at[i]) for i, (x, y) in enumerate(pairs)]
    for copy in copies:
        copy.start()
    return copies


def _early_kernel(where, own, other, upper, inverse, held, work, sems):
    core = where[1]
    copies = _fetch([(own, held.at[core]), (other, held.at[1 - core])], sems)
    for copy in copies:
        copy.wait()

    def block(slot):
        return jnp.stack([held[0, :, slot], held[1, :, slot]], 1).reshape(NB, NB)

    work[...] = block(0)

    def panel(k, _):
        u, v = _factor_block(work[...])
        upper[k] = u
        inverse[k] = v

        @pl.when(k == 0)
        def _():
            u01 = _nn(inverse[0], block(1))
            upper[2] = u01
            work[...] = block(2) - _tn(u01, u01)

        return 0

    lax.fori_loop(0, 2, panel, 0)


def _late_kernel(where, own, other, upper, inverse, over, diag, inverse_out, held, u, v, work, sems):
    core = where[1]
    copies = _fetch([(own, held.at[core]), (other, held.at[1 - core]), (upper.at[2], u), (inverse, v)], sems)
    for copy in copies:
        copy.wait()

    def block(i, j):
        slot = LATE.index((i, j))
        return jnp.stack([held[0, :, slot], held[1, :, slot]], 1).reshape(NB, NB)

    u02 = _nn(v[0], block(0, 2))
    u03 = _nt(v[0], block(3, 0))
    u12 = _nn(v[1], block(1, 2) - _tn(u[...], u02))
    u13 = _nn(v[1], block(1, 3) - _tn(u[...], u03))
    over[0], over[1], over[2], over[3] = u02, u03, u12, u13
    work[0] = block(2, 2) - _tn(u02, u02) - _tn(u12, u12)
    work[1] = block(2, 3) - _tn(u02, u03) - _tn(u12, u13)
    work[2] = block(3, 3) - _tn(u03, u03) - _tn(u13, u13)

    def panel(k, _):
        top, low = _factor_block(work[0])
        diag[k] = top
        inverse_out[k] = low

        @pl.when(k == 0)
        def _():
            u23 = _nn(inverse_out[0], work[1])
            over[4] = u23
            work[0] = work[2] - _tn(u23, u23)

        return 0

    lax.fori_loop(0, 2, panel, 0)


def _finish_kernel(
    where, kernel, own, other, top, early, inv01, over, diag, inv23,
    out, left, left_rows, top_cols, e, v, o, d, w, sems,
):
    row, core, col = where[0], where[1], where[2]
    pairs = [(own, left.at[core]), (other, left.at[1 - core]), (inv01, v.at[pl.ds(0, 2)]), (early, e)]
    pairs += [(inv23, v.at[pl.ds(2, 2)]), (over, o), (top.at[pl.ds(0, KP)], top_cols), (diag, d), (kernel, w)]
    copies = _fetch(pairs, sems)
    for copy in copies[:6]:
        copy.wait()
    offs = {(0, 1): e.at[2], (2, 3): o.at[4]}
    offs.update({at: o.at[i] for i, at in enumerate([(0, 2), (0, 3), (1, 2), (1, 3)])})
    for k in range(KP):
        part = jnp.concatenate([jnp.stack([left[0, :, k, l], left[1, :, k, l]], 1).reshape(NB, NB) for l in range(2)], 0)
        for j in range(k):
            part = part - _nn(left_rows[j], offs[j, k][...])
        left_rows[k] = _nt(part, v[k])
    for copy in copies[6:]:
        copy.wait()
    for k in range(KP):
        head = top_cols[k]
        for j in range(k):
            head = head - _tn(offs[j, k][...], top_cols[j])
        top_cols[k] = _nn(v[k], head)

    @pl.when(col >= KP)
    def _():
        total = w[...].reshape(2 * NB, NB)
        for k in range(KP):
            total = total - _nn(left_rows[k], top_cols[k])
        total = total.reshape(2, NB, NB)
        out[0] = jnp.where(row < KP, 0.0, total[0])
        out[1] = total[1]

    @pl.when(col < KP)
    def _():
        block = left_rows[col].reshape(2, NB, NB)
        out[0] = jnp.where(row < col, 0.0, block[0])
        out[1] = block[1]

    for k in range(KP):

        @pl.when((row == k) & (col == k))
        def _():
            out[0] = (e if k < 2 else d)[k % 2].T


def on_device(kernel):
    rows_axis, cols_axis = lax.axis_size("row"), lax.axis_size("col")
    row_index, col_index = lax.axis_index("row"), lax.axis_index("col")
    blocks = kernel.reshape(2, NB, NB)
    thin = NB // cols_axis

    cores = [list(range(core, cols_axis, 2)) for core in range(2)]

    def spread(x, groups, count):
        whole = jnp.broadcast_to(x[None], (count, *x.shape))
        return lax.all_to_all(whole, "col", 0, 0, axis_index_groups=groups)

    def swap(x):
        return lax.ppermute(x, "col", [(c, c ^ 1) for c in range(cols_axis)])

    top = lax.all_gather(blocks[0], "row")

    scattered = lax.all_to_all(blocks.reshape(2, cols_axis, thin, NB).swapaxes(0, 1), "col", 0, 0)[:KP]
    left_own = spread(scattered, cores, cols_axis // 2)
    left_other = swap(left_own)

    first = scattered[:, 0]
    mine = jnp.stack([lax.dynamic_index_in_dim(first, lax.rem(row_index + o, KP), 0, keepdims=False) for o in range(3)])
    far = [lax.ppermute(mine, "row", [(r, r + d) for r in range(KP)]) for d in range(KP, rows_axis, KP)]
    mine = jnp.where(row_index < KP, mine, sum(far))
    mine, left_own = lax.optimization_barrier((mine, left_own))
    turned = [mine]
    for o in (1, 2, -1):
        turned.append(lax.ppermute(mine, "row", [((r + o) % rows_axis, r) for r in range(rows_axis)]))
    turned = jnp.stack(turned)
    corner = lax.dynamic_slice_in_dim(
        jnp.concatenate([turned, turned]), lax.rem(KP * rows_axis - row_index, KP), KP, 0
    )
    held = {(r, (r + o) % KP): corner[r, o] for r in range(KP) for o in range(3)}

    order = EARLY + LATE
    own = spread(jnp.stack([held[at] for at in order]), cores, cols_axis // 2)
    early_own, late_own = own[:, : len(EARLY)], own[:, len(EARLY) :]
    early_other = swap(early_own)
    late_own, _ = lax.optimization_barrier((late_own, early_other))
    late_other = swap(late_own)

    place = jnp.stack(
        [row_index, lax.rem(col_index, 2), col_index]
    ).astype(jnp.int32)
    vmem = pl.BlockSpec(memory_space=pltpu.VMEM)
    smem = pl.BlockSpec(memory_space=pltpu.SMEM)
    anywhere = pl.BlockSpec(memory_space=pl.ANY)
    params = pltpu.CompilerParams(vmem_limit_bytes=60 * MIB)

    def tiles(*lead):
        return jax.ShapeDtypeStruct((*lead, NB, NB), F32)

    def scratch(*lead):
        return pltpu.VMEM((*lead, NB, NB), F32)

    def cost(us):
        return pl.CostEstimate(flops=us * 1_000_000_000, bytes_accessed=4_000_000, transcendentals=0)

    early, inv01 = pl.pallas_call(
        _early_kernel,
        out_shape=(tiles(3), tiles(2)),
        in_specs=[smem, anywhere, anywhere],
        out_specs=(vmem, vmem),
        scratch_shapes=[
            pltpu.VMEM((2, cols_axis // 2, len(EARLY), thin, NB), F32),
            scratch(),
            pltpu.SemaphoreType.DMA((2,)),
        ],
        compiler_params=params,
        cost_estimate=cost(20),
        name="early",
    )(place, early_own, early_other)
    over, diag, inv23 = pl.pallas_call(
        _late_kernel,
        out_shape=(tiles(5), tiles(2), tiles(2)),
        in_specs=[smem] + [anywhere] * 4,
        out_specs=(vmem, vmem, vmem),
        scratch_shapes=[
            pltpu.VMEM((2, cols_axis // 2, len(LATE), thin, NB), F32),
            scratch(),
            scratch(2),
            scratch(3),
            pltpu.SemaphoreType.DMA((4,)),
        ],
        compiler_params=params,
        cost_estimate=cost(24),
        name="late",
    )(place, late_own, late_other, early, inv01)
    out = pl.pallas_call(
        _finish_kernel,
        out_shape=tiles(2),
        in_specs=[smem] + [anywhere] * 9,
        out_specs=vmem,
        scratch_shapes=[
            pltpu.VMEM((2, cols_axis // 2, KP, 2, thin, NB), F32),
            pltpu.VMEM((KP, 2 * NB, NB), F32),
            scratch(KP),
            scratch(3),
            scratch(KP),
            scratch(5),
            scratch(2),
            scratch(2),
            pltpu.SemaphoreType.DMA((9,)),
        ],
        compiler_params=params,
        cost_estimate=cost(10),
        name="finish",
    )(place, blocks, left_own, left_other, top, early, inv01, over, diag, inv23)
    return out.reshape(kernel.shape)


def solution(mesh):
    spec = P(None, "row", None, "col")
    return jax.shard_map(
        on_device, mesh=mesh, in_specs=(spec,), out_specs=spec, check_vma=False
    )
```

time: 190 us -> 163 us (0.86)
  waiting for transfers between devices: 60.1 us -> 6.89 us
  blocking collectives: 18 us -> 38.9 us
  starting transfers between devices: 29.4 us -> 41.9 us
  Pallas kernels: 56.1 us -> 51 us
  local copies, waits for them, and re-layouts: 11.9 us -> 7.54 us
    all_to_all x3 -> x1, waiting for transfers between devices: 60.1 us -> 0.01 us  [spread(): return lax.all_to_all(whole, 'col', 0, 0, axis_index_groups=groups)]
    ppermute x0 -> x9, starting transfers between devices: none -> 36.1 us  [the longest x3 16.5 us: on_device(): lax.ppermute(mine, 'row', [(r, r + d) for r in range(KP)])]
    all_to_all x3 -> x1, starting transfers between devices: 29.4 us -> 5.84 us  [spread(): return lax.all_to_all(whole, 'col', 0, 0, axis_index_groups=groups)]
    all_to_all x1 -> x2, blocking collectives: 18 us -> 38.9 us  [the longest x1 21 us: spread(): return lax.all_to_all(whole, 'col', 0, 0, axis_index_groups=groups)]
    ppermute x0 -> x9, waiting for transfers between devices: none -> 6.85 us  [the longest x3 4.46 us: on_device(): lax.ppermute(mine, 'row', [((r + o) % rows_axis, r) for r in range(rows_a...]
    pallas_call x2 -> x3, Pallas kernels: 56.1 us -> 51 us  [the longest x1 19.8 us: on_device(): pl.pallas_call(_late_kernel, out_shape=(tiles(5), tiles(2), tiles(2)), in...]
    broadcast_in_dim x4 -> x2, local copies, waits for them, and re-layouts: 4.27 us -> 1.24 us  [spread(): whole = jnp.broadcast_to(x[None], (count, *x.shape))]
    unnamed x17 -> x26, local copies, waits for them, and re-layouts: 4.92 us -> 2.93 us
  transfers between devices with their start and end apart: 4 -> 11, of which waited for: 2 -> 3; matrix products, arithmetic and copies ran while one was open for 3% -> 2% of each run, Pallas kernels for 23% -> 22%
where the time goes in v2:
time: 163 us; the launch traced here: 161 us
  Pallas kernels  51 us (31%)
  starting transfers between devices  41.9 us (26%)
  blocking collectives  38.9 us (24%)
  between operations  13.8 us (8%)
  local copies, waits for them, and re-layouts  7.54 us (5%)
  waiting for transfers between devices  6.89 us (4%)
    all_to_all x1, blocking collectives, spread(): return lax.all_to_all(whole, 'col', 0, 0, axis_index_groups=groups)  21 us
    pallas_call x1, Pallas kernels, on_device(): pl.pallas_call(_late_kernel, out_shape=(tiles(5), tiles(2), tiles(2)), in...  19.8 us
    all_to_all x1, blocking collectives, on_device(): lax.all_to_all(blocks.reshape(2, cols_axis, thin, NB).swapaxes(0, 1), 'co...  18 us
    ppermute x3, starting transfers between devices, on_device(): lax.ppermute(mine, 'row', [(r, r + d) for r in range(KP)])  16.5 us
    pallas_call x1, Pallas kernels, on_device(): pl.pallas_call(_finish_kernel, out_shape=tiles(2), in_specs=[smem] + [any...  15.9 us
    pallas_call x1, Pallas kernels, on_device(): pl.pallas_call(_early_kernel, out_shape=(tiles(3), tiles(2)), in_specs=[s...  15.4 us
    ppermute x3, starting transfers between devices, on_device(): lax.ppermute(mine, 'row', [((r + o) % rows_axis, r) for r in range(rows_a...  13.4 us
    ppermute x3, starting transfers between devices, swap(): return lax.ppermute(x, 'col', [(c, c ^ 1) for c in range(cols_axis)])  6.23 us
  transfers between devices with their start and end apart: 11, of which 3 were waited for; matrix products, arithmetic and copies ran while one was open for 2% of the time, Pallas kernels for 22%

profile of v2, /device:TPU:6, one launch (start us, length us, event | category | flops | bytes accessed | tf_op | source)
XLA Modules:
  0.0 160.7 jit_solution(11080243687745566462)
XLA Ops:
  6.5 1.1 copy.15
  7.6 0.0 copy-start
  7.6 0.1 copy.14
  7.7 18.0 %all_to_all.15 = f32[32,2,8,256]{3,2,1,0:T(8,128)S(1)} all-to-all(f32[32,2,8,256]{3,2,1,0:T(8,128)S(1)} %bitcast.73), channel_id=1, replica_groups=mesh['row'=16,'col'=32] {'col'}, dimensions={0} | all-to-all | bytes 1048576 | tf_op jit(solution)/shard_map/all_to_all | solution.py:257
  25.7 1.1 broadcast_in_dim.4
  26.8 0.0 copy-done
  26.8 0.0 slice-start
  26.8 5.8 %all-to-all-start.1 = ((f32[16,4,2,8,256]{4,3,2,1,0:T(8,128)}), f32[16,4,2,8,256]{4,3,2,1,0:T(8,128)S(1)}, u32[]{:S(2)}, u32[]{:S(2)}) async-start(f32[16,4,2,8,256]{4,3,2,1,0:T(8,128)} %broadcast_in_dim.4), calls=%async_computation.1 | async-start | bytes 2097152 | tf_op jit(solution)/shard_map/all_to_all | solution.py:250
  32.6 0.0 all-gather.3.cloned.1.call-start
  32.7 7.9 %collective-permute-start = (f32[3,8,256]{2,1,0:T(8,128)S(1)}, f32[3,8,256]{2,1,0:T(8,128)S(1)}, u32[]{:S(2)}, u32[]{:S(2)}) collective-permute-start(f32[3,8,256]{2,1,0:T(8,128)S(1)} %pad_maximum_fusion), channel_id=1, source_target_pairs={{0,128},{32,160},{64,192},{96,224},{1,129},{33,161},{65,193},{97,2... | collective-permute-start | bytes 73736 | tf_op jit(solution)/shard_map/ppermute | solution.py:263
  40.6 7.3 %collective-permute-start.1 = (f32[3,8,256]{2,1,0:T(8,128)S(1)}, f32[3,8,256]{2,1,0:T(8,128)S(1)}, u32[]{:S(2)}, u32[]{:S(2)}) collective-permute-start(f32[3,8,256]{2,1,0:T(8,128)S(1)} %pad_maximum_fusion), channel_id=1, source_target_pairs={{0,256},{32,288},{64,320},{96,352},{1,257},{33,289},{65,321},{97,3... | collective-permute-start | bytes 73736 | tf_op jit(solution)/shard_map/ppermute | solution.py:263
  47.9 1.3 collective-permute-start.2
  49.2 0.0 slice-done
  49.2 0.7 copy.10
  49.9 0.0 all-gather.3.cloned.1.call-update
  50.0 0.0 collective-permute-done
  50.0 0.0 collective-permute-done.1
  50.0 2.4 %collective-permute-done.2 = f32[3,8,256]{2,1,0:T(8,128)S(1)} collective-permute-done((f32[3,8,256]{2,1,0:T(8,128)S(1)}, f32[3,8,256]{2,1,0:T(8,128)S(1)}, u32[]{:S(2)}, u32[]{:S(2)}) %collective-permute-start.2) | collective-permute-done | bytes 24608 | tf_op jit(solution)/shard_map/ppermute | solution.py:263
  52.4 0.0 all-to-all-done.1.own
  52.4 0.0 copy-start.1
  52.4 7.1 %collective-permute-start.4 = (f32[3,8,256]{2,1,0:T(8,128)S(1)}, f32[3,8,256]{2,1,0:T(8,128)S(1)}, u32[]{:S(2)}, u32[]{:S(2)}) collective-permute-start(f32[3,8,256]{2,1,0:T(8,128)S(1)} %add_select_fusion), channel_id=1, source_target_pairs={{32,0},{64,32},{96,64},{128,96},{160,128},{192,160},{224,192},{256... | collective-permute-start | bytes 73736 | tf_op jit(solution)/shard_map/ppermute | solution.py:268
  59.5 3.4 %collective-permute-start.5 = (f32[3,8,256]{2,1,0:T(8,128)S(1)}, f32[3,8,256]{2,1,0:T(8,128)S(1)}, u32[]{:S(2)}, u32[]{:S(2)}) collective-permute-start(f32[3,8,256]{2,1,0:T(8,128)S(1)} %add_select_fusion), channel_id=1, source_target_pairs={{64,0},{96,32},{128,64},{160,96},{192,128},{224,160},{256,192},{28... | collective-permute-start | bytes 73736 | tf_op jit(solution)/shard_map/ppermute | solution.py:268
  62.9 2.9 %collective-permute-start.6 = (f32[3,8,256]{2,1,0:T(8,128)S(1)}, f32[3,8,256]{2,1,0:T(8,128)S(1)}, u32[]{:S(2)}, u32[]{:S(2)}) collective-permute-start(f32[3,8,256]{2,1,0:T(8,128)S(1)} %add_select_fusion), channel_id=1, source_target_pairs={{480,0},{0,32},{32,64},{64,96},{96,128},{128,160},{160,192},{192,2... | collective-permute-start | bytes 73736 | tf_op jit(solution)/shard_map/ppermute | solution.py:268
  65.8 0.0 collective-permute-done.4
  65.8 0.4 collective-permute-done.5
  66.2 4.1 %collective-permute-done.6 = f32[3,8,256]{2,1,0:T(8,128)S(1)} collective-permute-done((f32[3,8,256]{2,1,0:T(8,128)S(1)}, f32[3,8,256]{2,1,0:T(8,128)S(1)}, u32[]{:S(2)}, u32[]{:S(2)}) %collective-permute-start.6) | collective-permute-done | bytes 24608 | tf_op jit(solution)/shard_map/ppermute | solution.py:268
  70.5 0.1 broadcast_in_dim.5
  70.7 21.0 %all_to_all.16 = f32[16,10,8,256]{3,2,1,0:T(8,128)S(1)} all-to-all(f32[16,10,8,256]{3,2,1,0:T(8,128)S(1)} %broadcast_in_dim.5), channel_id=1, replica_groups={{0,2,4,6,8,10,12,14,16,18,20,22,24,26,28,30},{1,3,5,7,9,11,13,15,17,19,..., dimensions={0} | all-to-all | bytes 2621440 | tf_op jit(solution)/shard_map/all_to_all | solution.py:250
  91.6 0.8 slice.67.own
  92.5 1.9 %collective-permute-start.7 = (f32[16,3,8,256]{3,2,1,0:T(8,128)}, f32[16,3,8,256]{3,2,1,0:T(8,128)}, u32[]{:S(2)}, u32[]{:S(2)}) collective-permute-start(f32[16,3,8,256]{3,2,1,0:T(8,128)} %slice.67.own), channel_id=1, source_target_pairs={{0,1},{1,0},{2,3},{3,2},{4,5},{5,4},{6,7},{7,6},{8,9},{9,8},{10,11... | collective-permute-start | bytes 1179656 | tf_op jit(solution)/shard_map/ppermute | solution.py:253
  94.4 0.6 pad_add_fusion.where
  95.0 0.0 copy-done.1
  95.0 2.4 %collective-permute-start.3 = (f32[16,4,2,8,256]{4,3,2,1,0:T(8,128)S(1)}, f32[16,4,2,8,256]{4,3,2,1,0:T(8,128)}, u32[]{:S(2)}, u32[]{:S(2)}) collective-permute-start(f32[16,4,2,8,256]{4,3,2,1,0:T(8,128)S(1)} %all-to-all-done.1.own), channel_id=1, source_target_pairs={{0,1},{1,0},{2,3},{3,2},{4,5},{5,4},{6,7},{7,6},{8,9},{9,8},{10,11... | collective-permute-start | bytes 3145736 | tf_op jit(solution)/shard_map/ppermute | solution.py:253
  97.4 0.1 slice.68.own
  97.4 0.0 copy-start.2
  97.4 0.0 collective-permute-done.7.other
  97.5 1.9 %collective-permute-start.8 = (f32[16,7,8,256]{3,2,1,0:T(8,128)S(1)}, f32[16,7,8,256]{3,2,1,0:T(8,128)S(1)}, u32[]{:S(2)}, u32[]{:S(2)}) collective-permute-start(f32[16,7,8,256]{3,2,1,0:T(8,128)S(1)} %slice.68.own), channel_id=1, source_target_pairs={{0,1},{1,0},{2,3},{3,2},{4,5},{5,4},{6,7},{7,6},{8,9},{9,8},{10,11... | collective-permute-start | bytes 2752520 | tf_op jit(solution)/shard_map/ppermute | solution.py:253
  99.4 15.4 %early.1 = (f32[3,256,256]{2,1,0:T(8,128)}, f32[2,256,256]{2,1,0:T(8,128)}) custom-call(s32[3]{0:T(128)} %pad_add_fusion.where, f32[16,3,8,256]{3,2,1,0:T(8,128)} %slice.67.own, f32[16,3,8,256]{3,2,1,0:T(8,128)} %collective-permute-done.7.other), custom_call_target="tpu_custom_call" | custom-call | flops 20000000000 | bytes 4000000 | tf_op jit(solution)/shard_map/early/pallas_call | solution.py:299
  114.8 0.0 copy-done.2
  114.8 0.0 collective-permute-done.8.other
  114.8 0.0 copy-start.3
  114.8 1.0 copy-done.3
  115.8 19.8 %late.1 = (f32[5,256,256]{2,1,0:T(8,128)}, f32[2,256,256]{2,1,0:T(8,128)}, f32[2,256,256]{2,1,0:T(8,128)}) custom-call(s32[3]{0:T(128)} %pad_add_fusion.where, f32[16,7,8,256]{3,2,1,0:T(8,128)} %copy-done.2, f32[16,7,8,256]{3,2,1,0:T(8,128)} %copy-done.3, f32[3,256,256]{2,1,0:T(8,128)} %get-tuple-element.15.upper.early, ...), custom_call_target="tpu_custom_call" | custom-call | flops 24000000000 | bytes 4000000 | tf_op jit(solution)/shard_map/late/pallas_call | solution.py:313
  135.6 0.0 collective-permute-done.3.other
  135.6 0.0 all-gather.3.cloned.1.call-done
  135.6 15.9 %finish.1 = f32[2,256,256]{2,1,0:T(8,128)} custom-call(s32[3]{0:T(128)} %pad_add_fusion.where, f32[2,256,256]{2,1,0:T(8,128)} %bitcast.72, f32[16,4,2,8,256]{4,3,2,1,0:T(8,128)} %copy-done.1, f32[16,4,2,8,256]{4,3,2,1,0:T(8,128)} %collective-permute-done.3.other, f32[16,256,256]{2,1,0:T(8,128)} %bitcast.75, f32[3,256,256]{2,1,0:T(8,128)} %get-tuple-element.15.upper.early, ...), custom_call_target="tpu_custom_call" | custom-call | flops 10000000000 | bytes 4000000 | tf_op jit(solution)/shard_map/finish/pallas_call | solution.py:329
  151.5 2.4 %copy.7 = f32[2,256,1,256]{3,2,1,0:T(1,128)} copy(f32[2,256,1,256]{3,1,0,2:T(8,128)} %bitcast.74) | data formatting | bytes 1048576 | tf_op jit(solution)/shard_map/reshape | solution.py:349
  (23 shorter events, 0.2 us)
Async XLA Ops:
  7.6 19.2 %copy-start = (f32[2,256,1,256]{3,1,2,0:T(8,128)}, f32[2,256,1,256]{3,1,2,0:T(8,128)S(1)}, u32[]{:S(2)}) copy-start(f32[2,256,1,256]{3,1,2,0:T(8,128)S(1)} %copy.15) | copy-start | bytes 1572868
  26.8 22.5 %slice-start = ((f32[2,256,1,256]{3,2,1,0:T(1,128)}), f32[1,256,1,256]{3,2,1,0:T(1,128)S(1)}, s32[]{:S(2)}) async-start(f32[2,256,1,256]{3,2,1,0:T(1,128)} %param.1), calls=%async_computation.4 | async-start | bytes 524288 | tf_op jit(solution)/shard_map/slice | solution.py:255
  26.8 25.6 %all-to-all-start.1 = ((f32[16,4,2,8,256]{4,3,2,1,0:T(8,128)}), f32[16,4,2,8,256]{4,3,2,1,0:T(8,128)S(1)}, u32[]{:S(2)}, u32[]{:S(2)}) async-start(f32[16,4,2,8,256]{4,3,2,1,0:T(8,128)} %broadcast_in_dim.4), calls=%async_computation.1 | async-start | bytes 2097152 | tf_op jit(solution)/shard_map/all_to_all | solution.py:250
  32.6 103.0 %all-gather.3.cloned.1.call-start = ((), (), s32[]{:S(2)}) async-start(), calls=%async_computation.3 | async-start | bytes 4456448 | tf_op jit(solution)/shard_map/all_gather | solution.py:255
  32.7 17.2 %collective-permute-start = (f32[3,8,256]{2,1,0:T(8,128)S(1)}, f32[3,8,256]{2,1,0:T(8,128)S(1)}, u32[]{:S(2)}, u32[]{:S(2)}) collective-permute-start(f32[3,8,256]{2,1,0:T(8,128)S(1)} %pad_maximum_fusion), channel_id=1, source_target_pairs={{0,128},{32,160},{64,192},{96,224},{1,129},{33,161},{65,193},{97,2... | collective-permute-start | bytes 73736 | tf_op jit(solution)/shard_map/ppermute | solution.py:263
  40.6 9.4 %collective-permute-start.1 = (f32[3,8,256]{2,1,0:T(8,128)S(1)}, f32[3,8,256]{2,1,0:T(8,128)S(1)}, u32[]{:S(2)}, u32[]{:S(2)}) collective-permute-start(f32[3,8,256]{2,1,0:T(8,128)S(1)} %pad_maximum_fusion), channel_id=1, source_target_pairs={{0,256},{32,288},{64,320},{96,352},{1,257},{33,289},{65,321},{97,3... | collective-permute-start | bytes 73736 | tf_op jit(solution)/shard_map/ppermute | solution.py:263
  47.9 4.4 %collective-permute-start.2 = (f32[3,8,256]{2,1,0:T(8,128)S(1)}, f32[3,8,256]{2,1,0:T(8,128)S(1)}, u32[]{:S(2)}, u32[]{:S(2)}) collective-permute-start(f32[3,8,256]{2,1,0:T(8,128)S(1)} %pad_maximum_fusion), channel_id=1, source_target_pairs={{0,384},{32,416},{64,448},{96,480},{1,385},{33,417},{65,449},{97,4... | collective-permute-start | bytes 73736 | tf_op jit(solution)/shard_map/ppermute | solution.py:263
  52.4 42.6 %copy-start.1 = (f32[16,4,2,8,256]{4,3,2,1,0:T(8,128)}, f32[16,4,2,8,256]{4,3,2,1,0:T(8,128)S(1)}, u32[]{:S(2)}) copy-start(f32[16,4,2,8,256]{4,3,2,1,0:T(8,128)S(1)} %all-to-all-done.1.own) | copy-start | bytes 3145732
  52.4 13.4 %collective-permute-start.4 = (f32[3,8,256]{2,1,0:T(8,128)S(1)}, f32[3,8,256]{2,1,0:T(8,128)S(1)}, u32[]{:S(2)}, u32[]{:S(2)}) collective-permute-start(f32[3,8,256]{2,1,0:T(8,128)S(1)} %add_select_fusion), channel_id=1, source_target_pairs={{32,0},{64,32},{96,64},{128,96},{160,128},{192,160},{224,192},{256... | collective-permute-start | bytes 73736 | tf_op jit(solution)/shard_map/ppermute | solution.py:268
  59.5 6.7 %collective-permute-start.5 = (f32[3,8,256]{2,1,0:T(8,128)S(1)}, f32[3,8,256]{2,1,0:T(8,128)S(1)}, u32[]{:S(2)}, u32[]{:S(2)}) collective-permute-start(f32[3,8,256]{2,1,0:T(8,128)S(1)} %add_select_fusion), channel_id=1, source_target_pairs={{64,0},{96,32},{128,64},{160,96},{192,128},{224,160},{256,192},{28... | collective-permute-start | bytes 73736 | tf_op jit(solution)/shard_map/ppermute | solution.py:268
  62.9 7.4 %collective-permute-start.6 = (f32[3,8,256]{2,1,0:T(8,128)S(1)}, f32[3,8,256]{2,1,0:T(8,128)S(1)}, u32[]{:S(2)}, u32[]{:S(2)}) collective-permute-start(f32[3,8,256]{2,1,0:T(8,128)S(1)} %add_select_fusion), channel_id=1, source_target_pairs={{480,0},{0,32},{32,64},{64,96},{96,128},{128,160},{160,192},{192,2... | collective-permute-start | bytes 73736 | tf_op jit(solution)/shard_map/ppermute | solution.py:268
  92.5 5.0 %collective-permute-start.7 = (f32[16,3,8,256]{3,2,1,0:T(8,128)}, f32[16,3,8,256]{3,2,1,0:T(8,128)}, u32[]{:S(2)}, u32[]{:S(2)}) collective-permute-start(f32[16,3,8,256]{3,2,1,0:T(8,128)} %slice.67.own), channel_id=1, source_target_pairs={{0,1},{1,0},{2,3},{3,2},{4,5},{5,4},{6,7},{7,6},{8,9},{9,8},{10,11... | collective-permute-start | bytes 1179656 | tf_op jit(solution)/shard_map/ppermute | solution.py:253
  95.0 40.7 %collective-permute-start.3 = (f32[16,4,2,8,256]{4,3,2,1,0:T(8,128)S(1)}, f32[16,4,2,8,256]{4,3,2,1,0:T(8,128)}, u32[]{:S(2)}, u32[]{:S(2)}) collective-permute-start(f32[16,4,2,8,256]{4,3,2,1,0:T(8,128)S(1)} %all-to-all-done.1.own), channel_id=1, source_target_pairs={{0,1},{1,0},{2,3},{3,2},{4,5},{5,4},{6,7},{7,6},{8,9},{9,8},{10,11... | collective-permute-start | bytes 3145736 | tf_op jit(solution)/shard_map/ppermute | solution.py:253
  97.4 17.4 %copy-start.2 = (f32[16,7,8,256]{3,2,1,0:T(8,128)}, f32[16,7,8,256]{3,2,1,0:T(8,128)S(1)}, u32[]{:S(2)}) copy-start(f32[16,7,8,256]{3,2,1,0:T(8,128)S(1)} %slice.68.own) | copy-start | bytes 2752516
  97.5 17.3 %collective-permute-start.8 = (f32[16,7,8,256]{3,2,1,0:T(8,128)S(1)}, f32[16,7,8,256]{3,2,1,0:T(8,128)S(1)}, u32[]{:S(2)}, u32[]{:S(2)}) collective-permute-start(f32[16,7,8,256]{3,2,1,0:T(8,128)S(1)} %slice.68.own), channel_id=1, source_target_pairs={{0,1},{1,0},{2,3},{3,2},{4,5},{5,4},{6,7},{7,6},{8,9},{9,8},{10,11... | collective-permute-start | bytes 2752520 | tf_op jit(solution)/shard_map/ppermute | solution.py:253
  114.8 1.0 copy-start.3
Sparse Core Ops, SparseCore 0:
  50.1 71.0 all-gather.2

commit v3 on v2

v3 whole, which is shorter than its diff:
```python
import jax
import jax.numpy as jnp
from jax import lax
from jax.experimental import pallas as pl
from jax.experimental.pallas import tpu as pltpu
from jax.sharding import PartitionSpec as P

KP = 4
GROUP = 8
NB = 256
F32 = jnp.float32
MIB = 1024 * 1024


def _dot(a, b, dims):
    return lax.dot_general(
        a, b, (dims, ((), ())), precision=lax.Precision.HIGHEST, preferred_element_type=F32
    )


def _nn(a, b):
    return _dot(a, b, ((1,), (0,)))


def _nt(a, b):
    return _dot(a, b, ((1,), (1,)))


def _tn(a, b):
    return _dot(a, b, ((0,), (0,)))


def _factor_tile(tile):
    count = tile.shape[0] // 8
    rows = [tile[8 * s : 8 * s + 8] for s in range(count)]
    lane = lax.broadcasted_iota(jnp.int32, (8, 128), 1)
    sub = lax.broadcasted_iota(jnp.int32, (8, 128), 0)

    def spread(x):
        return jnp.broadcast_to(x, (8, 128))

    def column(x, at):
        return jnp.take_along_axis(x, jnp.full((8, 128), at, jnp.int32), axis=1)

    upper, inverse = [], []
    own = [column(rows[0], k) for k in range(8)]
    for s in range(count):
        base = 8 * s
        stop = (s // GROUP + 1) * GROUP
        last = s + 1 == stop
        here = (lane >= base) & (lane < base + 8)
        ahead = [] if last else [column(rows[s], base + 8 + k) for k in range(8)]
        below = [] if last else [column(rows[s + 1], base + k) for k in range(8)]
        after = [] if last else [column(rows[s + 1], base + 8 + k) for k in range(8)]
        cols = {t: [column(rows[t], base + k) for k in range(8)] for t in range(s + 2, stop)}
        rows[s] = jnp.where(here, jnp.where(lane - base == sub, 1.0, 0.0), rows[s])
        for t in range(s + 1, stop):
            rows[t] = jnp.where(here, 0.0, rows[t])
        scales, pivots, pivot_rows = [], {}, []
        for j in range(8):
            scale = 1.0 / spread(own[j][j : j + 1, :])
            ratio = jnp.where(sub > j, own[j], 0.0) * scale
            for k in range(j + 1, 8):
                pivots[j, k] = spread(own[k][j : j + 1, :])
                own[k] = own[k] - ratio * pivots[j, k]
            pivot_row = spread(rows[s][j : j + 1, :])
            rows[s] = rows[s] - ratio * pivot_row
            scales.append(scale)
            pivot_rows.append(pivot_row)
            if not last:
                low = below[j] * scale
                for k in range(j + 1, 8):
                    below[k] = below[k] - low * pivots[j, k]
                for k in range(8):
                    pivot = spread(ahead[k][j : j + 1, :])
                    ahead[k] = ahead[k] - ratio * pivot
                    after[k] = after[k] - low * pivot
                rows[s + 1] = rows[s + 1] - low * pivot_row
        for t in range(s + 2, stop):
            other, row = cols[t], rows[t]
            for j in range(8):
                ratio = other[j] * scales[j]
                for k in range(j + 1, 8):
                    other[k] = other[k] - ratio * pivots[j, k]
                row = row - ratio * pivot_rows[j]
            rows[t] = row
        diag, square = own[0], own[0]
        for k in range(1, 8):
            diag = jnp.where(sub == k, own[k], diag)
            square = jnp.where(lane == base + k, own[k], square)
        root = lax.rsqrt(diag)
        square = jnp.where(sub <= lane - base, square, 0.0)
        upper.append(jnp.where(lane < base, 0.0, jnp.where(here, square, rows[s])) * root)
        inverse.append(jnp.where(lane < base + 8, rows[s], 0.0) * root)
        own = after
        if last and stop < count:
            low, high = 8 * (stop - GROUP), 8 * stop
            done = jnp.concatenate(upper[-GROUP:], 0)
            kept = jnp.where(lax.broadcasted_iota(jnp.int32, done.shape, 1) < high, jnp.concatenate(inverse[-GROUP:], 0), done)
            change = _tn(done, kept)
            for t in range(stop, count):
                inside = (lane >= low) & (lane < high)
                rows[t] = jnp.where(inside, 0.0, rows[t]) - change[8 * t : 8 * t + 8]
            own = [column(rows[stop], 8 * stop + k) for k in range(8)]
    return jnp.concatenate(upper, 0), jnp.concatenate(inverse, 0)


def _factor_block(block):
    h = NB // 2
    u11, v11 = _factor_tile(block[:h, :h])
    u12 = _nn(v11, block[:h, h:])
    u22, v22 = _factor_tile(block[h:, h:] - _tn(u12, u12))
    v21 = -_nn(v22, _tn(u12, v11))
    zero = jnp.zeros((h, h), F32)
    upper = jnp.concatenate([jnp.concatenate([u11, u12], 1), jnp.concatenate([zero, u22], 1)], 0)
    inverse = jnp.concatenate([jnp.concatenate([v11, zero], 1), jnp.concatenate([v21, v22], 1)], 0)
    return upper, inverse


EARLY = [(0, 0), (0, 1), (1, 1)]
LATE = [(1, 2), (2, 2), (2, 3), (3, 3), (3, 0), (0, 2), (1, 3)]


HALF = NB // 2


def _fetch(pairs, sems):
    copies = [pltpu.make_async_copy(x, y, sems.at[i]) for i, (x, y) in enumerate(pairs)]
    for copy in copies:
        copy.start()
    return copies


def _columns(half, rows):
    return pl.ds(half, rows, stride=2)


def _square(load):
    return jnp.concatenate([load(half).reshape(NB, HALF) for half in range(2)], 1)


def _paired(held, slot):
    def load(half):
        thin = held.shape[3] // 2
        return jnp.stack([held[core, :, slot, _columns(half, thin), :] for core in range(2)], 1)

    return _square(load)


def _early_kernel(own, other, upper, inverse, held, work, sems):
    core = lax.rem(lax.axis_index("col"), 2)
    count = len(EARLY)
    copies = _fetch([(own.at[:, pl.ds(0, count)], held.at[core]), (other, held.at[1 - core])], sems)
    for copy in copies:
        copy.wait()
    work[...] = _paired(held, 0)

    def panel(k, _):
        u, v = _factor_block(work[...])
        upper[k] = u
        inverse[k] = v

        @pl.when(k == 0)
        def _():
            u01 = _nn(inverse[0], _paired(held, 1))
            upper[2] = u01
            work[...] = _paired(held, 2) - _tn(u01, u01)

        return 0

    lax.fori_loop(0, 2, panel, 0)


def _late_kernel(own, other, upper, inverse, over, diag, inverse_out, held, u, v, sems):
    core = lax.rem(lax.axis_index("col"), 2)
    mine = own.at[:, pl.ds(len(EARLY), len(LATE))]
    copies = _fetch([(mine, held.at[core]), (other, held.at[1 - core]), (upper.at[2], u), (inverse, v)], sems)
    for copy in copies:
        copy.wait()

    def block(i, j):
        return _paired(held, LATE.index((i, j)))

    u02 = _nn(v[0], block(0, 2))
    u03 = _nt(v[0], block(3, 0))
    u12 = _nn(v[1], block(1, 2) - _tn(u[...], u02))
    u13 = _nn(v[1], block(1, 3) - _tn(u[...], u03))
    over[0], over[1], over[2], over[3] = u02, u03, u12, u13
    top, low = _factor_block(block(2, 2) - _tn(u02, u02) - _tn(u12, u12))
    u23 = _nn(low, block(2, 3) - _tn(u02, u03) - _tn(u12, u13))
    last = block(3, 3) - _tn(u03, u03) - _tn(u13, u13)
    diag[0], inverse_out[0], over[4] = top, low, u23
    diag[1], inverse_out[1] = _factor_block(last - _tn(u23, u23))


def _finish_kernel(
    kernel, left, top, early, inv01, over, diag, inv23,
    out, raw_left, raw_top, left_rows, top_cols, e, v, o, d, w, sems,
):
    row, col = lax.axis_index("row"), lax.axis_index("col")
    pairs = [(inv01, v.at[pl.ds(0, 2)]), (top.at[pl.ds(0, KP)], raw_top), (left, raw_left), (early, e), (over, o)]
    pairs += [(inv23, v.at[pl.ds(2, 2)]), (diag, d), (kernel, w)]
    copies = _fetch(pairs, sems)
    offs = {(0, 1): e.at[2], (2, 3): o.at[4]}
    offs.update({at: o.at[i] for i, at in enumerate([(0, 2), (0, 3), (1, 2), (1, 3)])})
    thin = raw_left.shape[3] // 2
    for copy in copies:
        copy.wait()
    for k in range(KP):
        head = _square(lambda half: raw_top[k, _columns(half, NB), :])
        parts = [_square(lambda half: raw_left[:, k, l, _columns(half, thin), :]) for l in range(2)]
        for j in range(k):
            head = head - _tn(offs[j, k][...], top_cols[j])
            parts = [parts[l] - _nn(left_rows[j, pl.ds(NB * l, NB)], offs[j, k][...]) for l in range(2)]
        top_cols[k] = _nn(v[k], head)
        for l in range(2):
            left_rows[k, pl.ds(NB * l, NB)] = _nt(parts[l], v[k])

    def store(l, block):
        for half in range(2):
            out[l, _columns(half, NB), :] = block[:, half * HALF : (half + 1) * HALF]

    @pl.when(col >= KP)
    def _():
        total = jnp.concatenate([_square(lambda half: w[l, _columns(half, NB), :]) for l in range(2)], 0)
        for k in range(KP):
            total = total - _nn(left_rows[k], top_cols[k])
        store(0, jnp.where(row < KP, 0.0, total[:NB]))
        store(1, total[NB:])

    @pl.when(col < KP)
    def _():
        block = left_rows[col]
        store(0, jnp.where(row < col, 0.0, block[:NB]))
        store(1, block[NB:])

    for k in range(KP):

        @pl.when((row == k) & (col == k))
        def _():
            store(0, (e if k < 2 else d)[k % 2].T)


VMEM = pl.BlockSpec(memory_space=pltpu.VMEM)
ANYWHERE = pl.BlockSpec(memory_space=pl.ANY)


def _tiles(*lead):
    return jax.ShapeDtypeStruct((*lead, NB, NB), F32)


def _scratch(*lead):
    return pltpu.VMEM((*lead, NB, NB), F32)


def _call(kernel, name, cost, copies, scratch, out_shape, operands):
    return pl.pallas_call(
        kernel,
        out_shape=out_shape,
        in_specs=[ANYWHERE] * len(operands),
        out_specs=jax.tree.map(lambda _: VMEM, out_shape),
        scratch_shapes=[*scratch, pltpu.SemaphoreType.DMA((copies,))],
        compiler_params=pltpu.CompilerParams(vmem_limit_bytes=60 * MIB),
        cost_estimate=pl.CostEstimate(flops=cost * 10**9, bytes_accessed=4_000_000, transcendentals=0),
        name=name,
    )(*operands)


def _early(own, other):
    held = pltpu.VMEM((2, *other.shape), F32)
    return _call(_early_kernel, "early", 12, 2, [held, _scratch()], (_tiles(3), _tiles(2)), (own, other))


def _late(own, other, upper, inverse):
    held = pltpu.VMEM((2, *other.shape), F32)
    return _call(
        _late_kernel,
        "late",
        16,
        4,
        [held, _scratch(), _scratch(2)],
        (_tiles(5), _tiles(2), _tiles(2)),
        (own, other, upper, inverse),
    )


def _finish(blocks, left, top, early, inv01, over, diag, inv23):
    scratch = [
        pltpu.VMEM(left.shape, F32),
        pltpu.VMEM((KP, *top.shape[1:]), F32),
        pltpu.VMEM((KP, 2 * NB, NB), F32),
        _scratch(KP),
        _scratch(3),
        _scratch(KP),
        _scratch(5),
        _scratch(2),
        pltpu.VMEM(blocks.shape, F32),
    ]
    return _call(
        _finish_kernel,
        "finish",
        10,
        8,
        scratch,
        jax.ShapeDtypeStruct(blocks.shape, F32),
        (blocks, left, top, early, inv01, over, diag, inv23),
    )


def on_device(kernel):
    rows_axis, cols_axis = lax.axis_size("row"), lax.axis_size("col")
    row_index, col_index = lax.axis_index("row"), lax.axis_index("col")
    blocks = kernel.reshape(2, 2 * NB, HALF)
    piece = (2 * NB // cols_axis, HALF)
    cores = [list(range(core, cols_axis, 2)) for core in range(2)]
    quads = [list(range(r, r + KP)) for r in range(0, rows_axis, KP)]

    def copies(x, count):
        return jnp.broadcast_to(x[None], (count, *x.shape))

    def spread(whole, axis, groups=None):
        return lax.all_to_all(whole, axis, 0, 0, axis_index_groups=groups)

    def swap(x):
        return lax.ppermute(x, "col", [(c, c ^ 1) for c in range(cols_axis)])

    cut = blocks.reshape(2, cols_axis, *piece).swapaxes(0, 1)
    scattered = lax.all_to_all(cut, "col", 0, 0)[:KP]

    lead, scattered = lax.optimization_barrier((blocks[0], scattered))
    top = lax.all_gather(lead, "row")

    first = scattered[:, 0]
    mine = jnp.stack([lax.dynamic_index_in_dim(first, lax.rem(row_index + o, KP), 0, keepdims=False) for o in range(3)])
    far = [lax.ppermute(mine, "row", [(r, r + d) for r in range(KP)]) for d in range(KP, rows_axis, KP)]
    mine = jnp.where(row_index < KP, mine, sum(far))
    mine, left = lax.optimization_barrier((mine, copies(scattered, cols_axis)))
    corner = spread(copies(mine, KP), "row", quads)

    order = [corner[r, (c - r) % KP] for r, c in EARLY + LATE]
    own = spread(copies(jnp.stack(order), cols_axis // 2), "col", cores)
    early_other = swap(own[:, : len(EARLY)])
    late_other = swap(own[:, len(EARLY) :])
    left, _ = lax.optimization_barrier((left, early_other))
    left = spread(left, "col")

    early, inv01 = _early(own, early_other)
    over, diag, inv23 = _late(own, late_other, early, inv01)
    out = _finish(blocks, left, top, early, inv01, over, diag, inv23)
    return out.reshape(kernel.shape)


def solution(mesh):
    spec = P(None, "row", None, "col")
    return jax.shard_map(
        on_device, mesh=mesh, in_specs=(spec,), out_specs=spec, check_vma=False
    )
```

time: 163 us -> 144 us (0.88)
  blocking collectives: 38.9 us -> 29.7 us
  starting transfers between devices: 41.9 us -> 35.6 us
  Pallas kernels: 51 us -> 45.4 us
  waiting for transfers between devices: 6.89 us -> 11.8 us
    ppermute x3 -> x0, starting transfers between devices: 13.4 us -> none  [on_device(): lax.ppermute(mine, 'row', [((r + o) % rows_axis, r) for r in range(rows_a...]
    all_to_all x1 -> x2, starting transfers between devices: 5.84 us -> 15.6 us  [the longest x1 9.55 us: on_device(): scattered = lax.all_to_all(cut, 'col', 0, 0)[:KP]]
    all_to_all x2, blocking collectives: 38.9 us -> 29.7 us  [spread(): return lax.all_to_all(whole, axis, 0, 0, axis_index_groups=groups)]
    all_to_all x1 -> x2, waiting for transfers between devices: 0.01 us -> 8.37 us  [the longest x1 8.37 us: on_device(): scattered = lax.all_to_all(cut, 'col', 0, 0)[:KP]]
    pallas_call x3, Pallas kernels: 51 us -> 45.4 us  [_call(): pl.pallas_call(kernel, out_shape=out_shape, in_specs=[ANYWHERE] * len(ope...]
    ppermute x3 -> x0, waiting for transfers between devices: 4.46 us -> none  [on_device(): lax.ppermute(mine, 'row', [((r + o) % rows_axis, r) for r in range(rows_a...]
    reshape x1 -> x0, local copies, waits for them, and re-layouts: 2.37 us -> none  [on_device(): return out.reshape(kernel.shape)]
    transpose x0 -> x1, local copies, waits for them, and re-layouts: none -> 1.97 us  [on_device(): cut = blocks.reshape(2, cols_axis, *piece).swapaxes(0, 1)]
  transfers between devices with their start and end apart: 11 -> 8, of which waited for: 3 -> 3; matrix products, arithmetic and copies ran while one was open for 2% -> 3% of each run, Pallas kernels for 22% -> 23%
where the time goes in v3:
time: 144 us; the launch traced here: 143 us
  Pallas kernels  45.4 us (32%)
  starting transfers between devices  35.6 us (25%)
  blocking collectives  29.7 us (21%)
  between operations  13.7 us (10%)
  waiting for transfers between devices  11.8 us (8%)
  local copies, waits for them, and re-layouts  7.1 us (5%)
    pallas_call x3, Pallas kernels, _call(): pl.pallas_call(kernel, out_shape=out_shape, in_specs=[ANYWHERE] * len(ope...  45.4 us
    all_to_all x2, blocking collectives, spread(): return lax.all_to_all(whole, axis, 0, 0, axis_index_groups=groups)  29.7 us
    ppermute x3, starting transfers between devices, on_device(): lax.ppermute(mine, 'row', [(r, r + d) for r in range(KP)])  15.7 us
    all_to_all x1, starting transfers between devices, on_device(): scattered = lax.all_to_all(cut, 'col', 0, 0)[:KP]  9.55 us
    all_to_all x1, waiting for transfers between devices, on_device(): scattered = lax.all_to_all(cut, 'col', 0, 0)[:KP]  8.37 us
    all_to_all x1, starting transfers between devices, spread(): return lax.all_to_all(whole, axis, 0, 0, axis_index_groups=groups)  6.04 us
    ppermute x2, starting transfers between devices, swap(): return lax.ppermute(x, 'col', [(c, c ^ 1) for c in range(cols_axis)])  4.32 us
    ppermute x3, waiting for transfers between devices, on_device(): lax.ppermute(mine, 'row', [(r, r + d) for r in range(KP)])  3.4 us
  transfers between devices with their start and end apart: 8, of which 3 were waited for; matrix products, arithmetic and copies ran while one was open for 3% of the time, Pallas kernels for 23%

profile of v3, /device:TPU:6, one launch (start us, length us, event | category | flops | bytes accessed | tf_op | source)
XLA Modules:
  0.0 143.3 jit_solution(13547553212772251383)
XLA Ops:
  6.5 0.0 copy-start.2
  6.5 2.0 %copy_bitcast_fusion = f32[32,2,16,128]{3,2,1,0:T(8,128)} fusion(f32[2,32,16,128]{3,2,1,0:T(8,128)} %bitcast.57), kind=kLoop, calls=%fused_computation | loop fusion | bytes 1048576 | tf_op jit(solution)/shard_map/transpose | solution.py:327
  8.5 9.6 %all-to-all-start = ((f32[32,2,16,128]{3,2,1,0:T(8,128)}), f32[32,2,16,128]{3,2,1,0:T(8,128)S(1)}, u32[]{:S(2)}, u32[]{:S(2)}) async-start(f32[32,2,16,128]{3,2,1,0:T(8,128)} %copy_bitcast_fusion), calls=%async_computation | async-start | bytes 1048576 | tf_op jit(solution)/shard_map/all_to_all | solution.py:328
  18.1 0.0 all-gather.3.cloned.1.call-start
  18.1 0.0 copy-done.2
  18.1 0.9 slice.46
  19.0 8.4 %all-to-all-done = f32[32,2,16,128]{3,2,1,0:T(8,128)S(1)} async-done(((f32[32,2,16,128]{3,2,1,0:T(8,128)}), f32[32,2,16,128]{3,2,1,0:T(8,128)S(1)}, u32[]{:S(2)}, u32[]{:S(2)}) %all-to-all-start) | async-done | bytes 524320 | tf_op jit(solution)/shard_map/all_to_all | solution.py:328
  27.4 0.0 all-gather.3.cloned.1.call-update
  27.5 7.1 %collective-permute-start = (f32[3,16,128]{2,1,0:T(8,128)S(1)}, f32[3,16,128]{2,1,0:T(8,128)S(1)}, u32[]{:S(2)}, u32[]{:S(2)}) collective-permute-start(f32[3,16,128]{2,1,0:T(8,128)S(1)} %pad_maximum_fusion), channel_id=1, source_target_pairs={{0,128},{32,160},{64,192},{96,224},{1,129},{33,161},{65,193},{97,2... | collective-permute-start | bytes 73736 | tf_op jit(solution)/shard_map/ppermute | solution.py:335
  34.6 7.3 %collective-permute-start.1 = (f32[3,16,128]{2,1,0:T(8,128)S(1)}, f32[3,16,128]{2,1,0:T(8,128)S(1)}, u32[]{:S(2)}, u32[]{:S(2)}) collective-permute-start(f32[3,16,128]{2,1,0:T(8,128)S(1)} %pad_maximum_fusion), channel_id=1, source_target_pairs={{0,256},{32,288},{64,320},{96,352},{1,257},{33,289},{65,321},{97,3... | collective-permute-start | bytes 73736 | tf_op jit(solution)/shard_map/ppermute | solution.py:335
  41.9 1.3 collective-permute-start.2
  43.2 0.0 collective-permute-done
  43.2 0.2 collective-permute-done.1
  43.4 3.2 %collective-permute-done.2 = f32[3,16,128]{2,1,0:T(8,128)S(1)} collective-permute-done((f32[3,16,128]{2,1,0:T(8,128)S(1)}, f32[3,16,128]{2,1,0:T(8,128)S(1)}, u32[]{:S(2)}, u32[]{:S(2)}) %collective-permute-start.2) | collective-permute-done | bytes 24608 | tf_op jit(solution)/shard_map/ppermute | solution.py:335
  46.6 1.6 %broadcast_in_dim.6 = f32[32,4,2,16,128]{4,3,2,1,0:T(8,128)} broadcast(f32[4,2,16,128]{3,2,1,0:T(8,128)S(1)} %slice.61), dimensions={1,2,3,4} | broadcast | bytes 2162688 | tf_op jit(solution)/shard_map/broadcast_in_dim | solution.py:319
  48.3 8.3 %all_to_all.20 = f32[4,3,16,128]{3,2,1,0:T(8,128)S(1)} all-to-all(f32[4,3,16,128]{3,2,1,0:T(8,128)S(1)} %broadcast_in_dim.7), channel_id=1, replica_groups={{0,32,64,96},{128,160,192,224},{256,288,320,352},{384,416,448,480},{1,3..., dimensions={0} | all-to-all | bytes 196608 | tf_op jit(solution)/shard_map/all_to_all | solution.py:322
  56.6 0.1 broadcast_in_dim.8
  56.8 21.3 %all_to_all.21.own = f32[16,10,16,128]{3,2,1,0:T(8,128)S(1)} all-to-all(f32[16,10,16,128]{3,2,1,0:T(8,128)S(1)} %broadcast_in_dim.8), channel_id=1, replica_groups={{0,2,4,6,8,10,12,14,16,18,20,22,24,26,28,30},{1,3,5,7,9,11,13,15,17,19,..., dimensions={0} | all-to-all | bytes 2621440 | tf_op jit(solution)/shard_map/all_to_all | solution.py:322
  78.1 0.0 copy-start
  78.2 1.9 %collective-permute-start.3 = (f32[16,3,16,128]{3,2,1,0:T(8,128)S(1)}, f32[16,3,16,128]{3,2,1,0:T(8,128)}, u32[]{:S(2)}, u32[]{:S(2)}) collective-permute-start(f32[16,3,16,128]{3,2,1,0:T(8,128)S(1)} %slice.72), channel_id=1, source_target_pairs={{0,1},{1,0},{2,3},{3,2},{4,5},{5,4},{6,7},{7,6},{8,9},{9,8},{10,11... | collective-permute-start | bytes 1179656 | tf_op jit(solution)/shard_map/ppermute | solution.py:325
  80.1 1.1 slice.73
  81.2 2.4 %collective-permute-start.4 = (f32[16,7,16,128]{3,2,1,0:T(8,128)}, f32[16,7,16,128]{3,2,1,0:T(8,128)}, u32[]{:S(2)}, u32[]{:S(2)}) collective-permute-start(f32[16,7,16,128]{3,2,1,0:T(8,128)} %slice.73), channel_id=1, source_target_pairs={{0,1},{1,0},{2,3},{3,2},{4,5},{5,4},{6,7},{7,6},{8,9},{9,8},{10,11... | collective-permute-start | bytes 2752520 | tf_op jit(solution)/shard_map/ppermute | solution.py:325
  83.6 0.0 collective-permute-done.3.other
  83.6 0.0 copy-done
  83.6 6.0 %all-to-all-start.3 = ((f32[32,4,2,16,128]{4,3,2,1,0:T(8,128)}), f32[32,4,2,16,128]{4,3,2,1,0:T(8,128)S(1)}, u32[]{:S(2)}, u32[]{:S(2)}) async-start(f32[32,4,2,16,128]{4,3,2,1,0:T(8,128)} %broadcast_in_dim.6), calls=%async_computation.3 | async-start | bytes 4194304 | tf_op jit(solution)/shard_map/all_to_all | solution.py:322
  89.6 14.7 %early.1 = (f32[3,256,256]{2,1,0:T(8,128)}, f32[2,256,256]{2,1,0:T(8,128)}) custom-call(f32[16,10,16,128]{3,2,1,0:T(8,128)} %copy-done, f32[16,3,16,128]{3,2,1,0:T(8,128)} %collective-permute-done.3.other), custom_call_target="tpu_custom_call" | custom-call | flops 12000000000 | bytes 4000000 | tf_op jit(solution)/shard_map/early/pallas_call | solution.py:257
  104.4 0.0 collective-permute-done.4.other
  104.4 17.9 %late.1 = (f32[5,256,256]{2,1,0:T(8,128)}, f32[2,256,256]{2,1,0:T(8,128)}, f32[2,256,256]{2,1,0:T(8,128)}) custom-call(f32[16,10,16,128]{3,2,1,0:T(8,128)} %copy-done, f32[16,7,16,128]{3,2,1,0:T(8,128)} %collective-permute-done.4.other, f32[3,256,256]{2,1,0:T(8,128)} %get-tuple-element.20.upper.early, f32[2,256,256]{2,1,0:T(8,128)} %get-tuple-element.21.inverse.inv01), custom_call_target="tpu_custom_call" | custom-call | flops 16000000000 | bytes 4000000 | tf_op jit(solution)/shard_map/late/pallas_call | solution.py:257
  122.3 0.0 all-to-all-done.3.left
  122.3 0.0 copy-start.1
  122.4 0.0 all-gather.3.cloned.1.call-done
  122.4 1.3 copy-done.1
  123.7 12.7 %finish.1 = f32[2,512,128]{2,1,0:T(8,128)} custom-call(f32[2,512,128]{2,1,0:T(8,128)} %bitcast.58, f32[32,4,2,16,128]{4,3,2,1,0:T(8,128)} %copy-done.1, f32[16,512,128]{2,1,0:T(8,128)} %bitcast.60, f32[3,256,256]{2,1,0:T(8,128)} %get-tuple-element.20.upper.early, f32[2,256,256]{2,1,0:T(8,128)} %get-tuple-element.21.inverse.inv01, ...), custom_call_target="tpu_custom_call" | custom-call | flops 10000000000 | bytes 4000000 | tf_op jit(solution)/shard_map/finish/pallas_call | solution.py:257
  (17 shorter events, 0.1 us)
Async XLA Ops:
  6.5 11.6 %copy-start.2 = (f32[2,256,1,256]{3,2,1,0:T(1,128)S(1)}, f32[2,256,1,256]{3,2,1,0:T(1,128)}, u32[]{:S(2)}) copy-start(f32[2,256,1,256]{3,2,1,0:T(1,128)} %param.1) | copy-start | bytes 1572868
  8.5 18.9 %all-to-all-start = ((f32[32,2,16,128]{3,2,1,0:T(8,128)}), f32[32,2,16,128]{3,2,1,0:T(8,128)S(1)}, u32[]{:S(2)}, u32[]{:S(2)}) async-start(f32[32,2,16,128]{3,2,1,0:T(8,128)} %copy_bitcast_fusion), calls=%async_computation | async-start | bytes 1048576 | tf_op jit(solution)/shard_map/all_to_all | solution.py:328
  18.1 104.3 %all-gather.3.cloned.1.call-start = ((), (), s32[]{:S(2)}) async-start(), calls=%async_computation.4 | async-start | bytes 4456448 | tf_op jit(solution)/shard_map/all_gather | solution.py:331
  27.5 15.7 %collective-permute-start = (f32[3,16,128]{2,1,0:T(8,128)S(1)}, f32[3,16,128]{2,1,0:T(8,128)S(1)}, u32[]{:S(2)}, u32[]{:S(2)}) collective-permute-start(f32[3,16,128]{2,1,0:T(8,128)S(1)} %pad_maximum_fusion), channel_id=1, source_target_pairs={{0,128},{32,160},{64,192},{96,224},{1,129},{33,161},{65,193},{97,2... | collective-permute-start | bytes 73736 | tf_op jit(solution)/shard_map/ppermute | solution.py:335
  34.6 8.8 %collective-permute-start.1 = (f32[3,16,128]{2,1,0:T(8,128)S(1)}, f32[3,16,128]{2,1,0:T(8,128)S(1)}, u32[]{:S(2)}, u32[]{:S(2)}) collective-permute-start(f32[3,16,128]{2,1,0:T(8,128)S(1)} %pad_maximum_fusion), channel_id=1, source_target_pairs={{0,256},{32,288},{64,320},{96,352},{1,257},{33,289},{65,321},{97,3... | collective-permute-start | bytes 73736 | tf_op jit(solution)/shard_map/ppermute | solution.py:335
  41.9 4.7 %collective-permute-start.2 = (f32[3,16,128]{2,1,0:T(8,128)S(1)}, f32[3,16,128]{2,1,0:T(8,128)S(1)}, u32[]{:S(2)}, u32[]{:S(2)}) collective-permute-start(f32[3,16,128]{2,1,0:T(8,128)S(1)} %pad_maximum_fusion), channel_id=1, source_target_pairs={{0,384},{32,416},{64,448},{96,480},{1,385},{33,417},{65,449},{97,4... | collective-permute-start | bytes 73736 | tf_op jit(solution)/shard_map/ppermute | solution.py:335
  78.1 5.5 %copy-start = (f32[16,10,16,128]{3,2,1,0:T(8,128)}, f32[16,10,16,128]{3,2,1,0:T(8,128)S(1)}, u32[]{:S(2)}) copy-start(f32[16,10,16,128]{3,2,1,0:T(8,128)S(1)} %all_to_all.21.own) | copy-start | bytes 3932164
  78.2 5.4 %collective-permute-start.3 = (f32[16,3,16,128]{3,2,1,0:T(8,128)S(1)}, f32[16,3,16,128]{3,2,1,0:T(8,128)}, u32[]{:S(2)}, u32[]{:S(2)}) collective-permute-start(f32[16,3,16,128]{3,2,1,0:T(8,128)S(1)} %slice.72), channel_id=1, source_target_pairs={{0,1},{1,0},{2,3},{3,2},{4,5},{5,4},{6,7},{7,6},{8,9},{9,8},{10,11... | collective-permute-start | bytes 1179656 | tf_op jit(solution)/shard_map/ppermute | solution.py:325
  81.2 23.2 %collective-permute-start.4 = (f32[16,7,16,128]{3,2,1,0:T(8,128)}, f32[16,7,16,128]{3,2,1,0:T(8,128)}, u32[]{:S(2)}, u32[]{:S(2)}) collective-permute-start(f32[16,7,16,128]{3,2,1,0:T(8,128)} %slice.73), channel_id=1, source_target_pairs={{0,1},{1,0},{2,3},{3,2},{4,5},{5,4},{6,7},{7,6},{8,9},{9,8},{10,11... | collective-permute-start | bytes 2752520 | tf_op jit(solution)/shard_map/ppermute | solution.py:325
  83.6 38.7 %all-to-all-start.3 = ((f32[32,4,2,16,128]{4,3,2,1,0:T(8,128)}), f32[32,4,2,16,128]{4,3,2,1,0:T(8,128)S(1)}, u32[]{:S(2)}, u32[]{:S(2)}) async-start(f32[32,4,2,16,128]{4,3,2,1,0:T(8,128)} %broadcast_in_dim.6), calls=%async_computation.3 | async-start | bytes 4194304 | tf_op jit(solution)/shard_map/all_to_all | solution.py:322
  122.3 1.4 copy-start.1
Sparse Core Ops, SparseCore 0:
  27.5 80.9 all-gather.2

commit v4 on v3

--- a/solution.py
+++ b/solution.py
@@ -150,7 +150,7 @@
 def _early_kernel(own, other, upper, inverse, held, work, sems):
     core = lax.rem(lax.axis_index("col"), 2)
     count = len(EARLY)
-    copies = _fetch([(own.at[:, pl.ds(0, count)], held.at[core]), (other, held.at[1 - core])], sems)
+    copies = _fetch([(x.at[:, pl.ds(0, count)], held.at[at]) for x, at in ((own, core), (other, 1 - core))], sems)
     for copy in copies:
         copy.wait()
     work[...] = _paired(held, 0)
@@ -173,8 +173,8 @@
 
 def _late_kernel(own, other, upper, inverse, over, diag, inverse_out, held, u, v, sems):
     core = lax.rem(lax.axis_index("col"), 2)
-    mine = own.at[:, pl.ds(len(EARLY), len(LATE))]
-    copies = _fetch([(mine, held.at[core]), (other, held.at[1 - core]), (upper.at[2], u), (inverse, v)], sems)
+    pairs = [(x.at[:, pl.ds(len(EARLY), len(LATE))], held.at[at]) for x, at in ((own, core), (other, 1 - core))]
+    copies = _fetch([*pairs, (upper.at[2], u), (inverse, v)], sems)
     for copy in copies:
         copy.wait()
 
@@ -267,12 +267,12 @@
 
 
 def _early(own, other):
-    held = pltpu.VMEM((2, *other.shape), F32)
+    held = pltpu.VMEM((2, own.shape[0], len(EARLY), *own.shape[2:]), F32)
     return _call(_early_kernel, "early", 12, 2, [held, _scratch()], (_tiles(3), _tiles(2)), (own, other))
 
 
 def _late(own, other, upper, inverse):
-    held = pltpu.VMEM((2, *other.shape), F32)
+    held = pltpu.VMEM((2, own.shape[0], len(LATE), *own.shape[2:]), F32)
     return _call(
         _late_kernel,
         "late",
@@ -339,13 +339,12 @@
 
     order = [corner[r, (c - r) % KP] for r, c in EARLY + LATE]
     own = spread(copies(jnp.stack(order), cols_axis // 2), "col", cores)
-    early_other = swap(own[:, : len(EARLY)])
-    late_other = swap(own[:, len(EARLY) :])
-    left, _ = lax.optimization_barrier((left, early_other))
+    other = swap(own)
+    left, _ = lax.optimization_barrier((left, own))
     left = spread(left, "col")
 
-    early, inv01 = _early(own, early_other)
-    over, diag, inv23 = _late(own, late_other, early, inv01)
+    early, inv01 = _early(own, other)
+    over, diag, inv23 = _late(own, other, early, inv01)
     out = _finish(blocks, left, top, early, inv01, over, diag, inv23)
     return out.reshape(kernel.shape)
 

time: 144 us -> 141 us (0.979)
  starting transfers between devices: 35.6 us -> 33.3 us
    ppermute x2 -> x1, starting transfers between devices: 4.32 us -> 1.91 us  [swap(): return lax.ppermute(x, 'col', [(c, c ^ 1) for c in range(cols_axis)])]
  transfers between devices with their start and end apart: 8 -> 7, of which waited for: 3 -> 3; matrix products, arithmetic and copies ran while one was open for 3% -> 2% of each run, Pallas kernels for 23% -> 23%
where the time goes in v4:
time: 141 us; the launch traced here: 140 us
  Pallas kernels  45.4 us (32%)
  starting transfers between devices  33.3 us (24%)
  blocking collectives  30.2 us (21%)
  between operations  13.6 us (10%)
  waiting for transfers between devices  11.6 us (8%)
  local copies, waits for them, and re-layouts  6 us (4%)
    pallas_call x3, Pallas kernels, _call(): pl.pallas_call(kernel, out_shape=out_shape, in_specs=[ANYWHERE] * len(ope...  45.4 us
    all_to_all x2, blocking collectives, spread(): return lax.all_to_all(whole, axis, 0, 0, axis_index_groups=groups)  30.2 us
    ppermute x3, starting transfers between devices, on_device(): lax.ppermute(mine, 'row', [(r, r + d) for r in range(KP)])  15.7 us
    all_to_all x1, starting transfers between devices, on_device(): scattered = lax.all_to_all(cut, 'col', 0, 0)[:KP]  9.55 us
    all_to_all x1, waiting for transfers between devices, on_device(): scattered = lax.all_to_all(cut, 'col', 0, 0)[:KP]  8.33 us
    all_to_all x1, starting transfers between devices, spread(): return lax.all_to_all(whole, axis, 0, 0, axis_index_groups=groups)  6.08 us
    ppermute x3, waiting for transfers between devices, on_device(): lax.ppermute(mine, 'row', [(r, r + d) for r in range(KP)])  3.21 us
  transfers between devices with their start and end apart: 7, of which 3 were waited for; matrix products, arithmetic and copies ran while one was open for 2% of the time, Pallas kernels for 23%

profile of v4, /device:TPU:6, one launch (start us, length us, event | category | flops | bytes accessed | tf_op | source)
XLA Modules:
  0.0 140.2 jit_solution(18196922552582281785)
XLA Ops:
  6.5 0.0 copy-start.2
  6.5 2.0 %copy_bitcast_fusion = f32[32,2,16,128]{3,2,1,0:T(8,128)} fusion(f32[2,32,16,128]{3,2,1,0:T(8,128)} %bitcast.57), kind=kLoop, calls=%fused_computation | loop fusion | bytes 1048576 | tf_op jit(solution)/shard_map/transpose | solution.py:327
  8.5 9.6 %all-to-all-start = ((f32[32,2,16,128]{3,2,1,0:T(8,128)}), f32[32,2,16,128]{3,2,1,0:T(8,128)S(1)}, u32[]{:S(2)}, u32[]{:S(2)}) async-start(f32[32,2,16,128]{3,2,1,0:T(8,128)} %copy_bitcast_fusion), calls=%async_computation | async-start | bytes 1048576 | tf_op jit(solution)/shard_map/all_to_all | solution.py:328
  18.1 0.0 all-gather.3.cloned.1.call-start
  18.1 0.0 copy-done.2
  18.1 0.9 slice.40
  19.1 8.3 %all-to-all-done = f32[32,2,16,128]{3,2,1,0:T(8,128)S(1)} async-done(((f32[32,2,16,128]{3,2,1,0:T(8,128)}), f32[32,2,16,128]{3,2,1,0:T(8,128)S(1)}, u32[]{:S(2)}, u32[]{:S(2)}) %all-to-all-start) | async-done | bytes 524320 | tf_op jit(solution)/shard_map/all_to_all | solution.py:328
  27.4 7.1 %collective-permute-start = (f32[3,16,128]{2,1,0:T(8,128)S(1)}, f32[3,16,128]{2,1,0:T(8,128)S(1)}, u32[]{:S(2)}, u32[]{:S(2)}) collective-permute-start(f32[3,16,128]{2,1,0:T(8,128)S(1)} %pad_maximum_fusion), channel_id=1, source_target_pairs={{0,128},{32,160},{64,192},{96,224},{1,129},{33,161},{65,193},{97,2... | collective-permute-start | bytes 73736 | tf_op jit(solution)/shard_map/ppermute | solution.py:335
  34.6 7.3 %collective-permute-start.1 = (f32[3,16,128]{2,1,0:T(8,128)S(1)}, f32[3,16,128]{2,1,0:T(8,128)S(1)}, u32[]{:S(2)}, u32[]{:S(2)}) collective-permute-start(f32[3,16,128]{2,1,0:T(8,128)S(1)} %pad_maximum_fusion), channel_id=1, source_target_pairs={{0,256},{32,288},{64,320},{96,352},{1,257},{33,289},{65,321},{97,3... | collective-permute-start | bytes 73736 | tf_op jit(solution)/shard_map/ppermute | solution.py:335
  41.9 1.3 collective-permute-start.2
  43.2 0.0 all-gather.3.cloned.1.call-update
  43.2 0.0 collective-permute-done
  43.2 0.2 collective-permute-done.1
  43.4 3.0 %collective-permute-done.2 = f32[3,16,128]{2,1,0:T(8,128)S(1)} collective-permute-done((f32[3,16,128]{2,1,0:T(8,128)S(1)}, f32[3,16,128]{2,1,0:T(8,128)S(1)}, u32[]{:S(2)}, u32[]{:S(2)}) %collective-permute-start.2) | collective-permute-done | bytes 24608 | tf_op jit(solution)/shard_map/ppermute | solution.py:335
  46.4 1.6 %broadcast_in_dim.6 = f32[32,4,2,16,128]{4,3,2,1,0:T(8,128)} broadcast(f32[4,2,16,128]{3,2,1,0:T(8,128)S(1)} %slice.53), dimensions={1,2,3,4} | broadcast | bytes 2162688 | tf_op jit(solution)/shard_map/broadcast_in_dim | solution.py:319
  48.0 8.7 %all_to_all.20 = f32[4,3,16,128]{3,2,1,0:T(8,128)S(1)} all-to-all(f32[4,3,16,128]{3,2,1,0:T(8,128)S(1)} %broadcast_in_dim.7), channel_id=1, replica_groups={{0,32,64,96},{128,160,192,224},{256,288,320,352},{384,416,448,480},{1,3..., dimensions={0} | all-to-all | bytes 196608 | tf_op jit(solution)/shard_map/all_to_all | solution.py:322
  56.9 0.1 broadcast_in_dim.8
  57.0 21.5 %all_to_all.21.own = f32[16,10,16,128]{3,2,1,0:T(8,128)S(1)} all-to-all(f32[16,10,16,128]{3,2,1,0:T(8,128)S(1)} %broadcast_in_dim.8), channel_id=1, replica_groups={{0,2,4,6,8,10,12,14,16,18,20,22,24,26,28,30},{1,3,5,7,9,11,13,15,17,19,..., dimensions={0} | all-to-all | bytes 2621440 | tf_op jit(solution)/shard_map/all_to_all | solution.py:322
  78.5 0.0 copy-start.1
  78.5 1.9 %collective-permute-start.3 = (f32[16,10,16,128]{3,2,1,0:T(8,128)S(1)}, f32[16,10,16,128]{3,2,1,0:T(8,128)}, u32[]{:S(2)}, u32[]{:S(2)}) collective-permute-start(f32[16,10,16,128]{3,2,1,0:T(8,128)S(1)} %all_to_all.21.own), channel_id=1, source_target_pairs={{0,1},{1,0},{2,3},{3,2},{4,5},{5,4},{6,7},{7,6},{8,9},{9,8},{10,11... | collective-permute-start | bytes 3932168 | tf_op jit(solution)/shard_map/ppermute | solution.py:325
  80.4 0.0 copy-done.1
  80.4 6.1 %all-to-all-start.3 = ((f32[32,4,2,16,128]{4,3,2,1,0:T(8,128)}), f32[32,4,2,16,128]{4,3,2,1,0:T(8,128)S(1)}, u32[]{:S(2)}, u32[]{:S(2)}) async-start(f32[32,4,2,16,128]{4,3,2,1,0:T(8,128)} %broadcast_in_dim.6), calls=%async_computation.3 | async-start | bytes 4194304 | tf_op jit(solution)/shard_map/all_to_all | solution.py:322
  86.5 0.0 collective-permute-done.3.other
  86.5 14.7 %early.1 = (f32[3,256,256]{2,1,0:T(8,128)}, f32[2,256,256]{2,1,0:T(8,128)}) custom-call(f32[16,10,16,128]{3,2,1,0:T(8,128)} %copy-done.1, f32[16,10,16,128]{3,2,1,0:T(8,128)} %collective-permute-done.3.other), custom_call_target="tpu_custom_call" | custom-call | flops 12000000000 | bytes 4000000 | tf_op jit(solution)/shard_map/early/pallas_call | solution.py:257
  101.3 18.0 %late.1 = (f32[5,256,256]{2,1,0:T(8,128)}, f32[2,256,256]{2,1,0:T(8,128)}, f32[2,256,256]{2,1,0:T(8,128)}) custom-call(f32[16,10,16,128]{3,2,1,0:T(8,128)} %copy-done.1, f32[16,10,16,128]{3,2,1,0:T(8,128)} %collective-permute-done.3.other, f32[3,256,256]{2,1,0:T(8,128)} %get-tuple-element.20.upper.early, f32[2,256,256]{2,1,0:T(8,128)} %get-tuple-element.21.inverse.inv01), custom_call_target="tpu_custom_call" | custom-call | flops 16000000000 | bytes 4000000 | tf_op jit(solution)/shard_map/late/pallas_call | solution.py:257
  119.3 0.0 all-to-all-done.3.left
  119.3 0.0 copy-start
  119.3 0.0 all-gather.3.cloned.1.call-done
  119.3 1.3 copy-done
  120.6 12.7 %finish.1 = f32[2,512,128]{2,1,0:T(8,128)} custom-call(f32[2,512,128]{2,1,0:T(8,128)} %bitcast.58, f32[32,4,2,16,128]{4,3,2,1,0:T(8,128)} %copy-done, f32[16,512,128]{2,1,0:T(8,128)} %bitcast.60, f32[3,256,256]{2,1,0:T(8,128)} %get-tuple-element.20.upper.early, f32[2,256,256]{2,1,0:T(8,128)} %get-tuple-element.21.inverse.inv01, ...), custom_call_target="tpu_custom_call" | custom-call | flops 10000000000 | bytes 4000000 | tf_op jit(solution)/shard_map/finish/pallas_call | solution.py:257
  (16 shorter events, 0.1 us)
Async XLA Ops:
  6.5 11.6 %copy-start.2 = (f32[2,256,1,256]{3,2,1,0:T(1,128)S(1)}, f32[2,256,1,256]{3,2,1,0:T(1,128)}, u32[]{:S(2)}) copy-start(f32[2,256,1,256]{3,2,1,0:T(1,128)} %param.1) | copy-start | bytes 1572868
  8.5 18.9 %all-to-all-start = ((f32[32,2,16,128]{3,2,1,0:T(8,128)}), f32[32,2,16,128]{3,2,1,0:T(8,128)S(1)}, u32[]{:S(2)}, u32[]{:S(2)}) async-start(f32[32,2,16,128]{3,2,1,0:T(8,128)} %copy_bitcast_fusion), calls=%async_computation | async-start | bytes 1048576 | tf_op jit(solution)/shard_map/all_to_all | solution.py:328
  18.1 101.2 %all-gather.3.cloned.1.call-start = ((), (), s32[]{:S(2)}) async-start(), calls=%async_computation.4 | async-start | bytes 4456448 | tf_op jit(solution)/shard_map/all_gather | solution.py:331
  27.4 15.8 %collective-permute-start = (f32[3,16,128]{2,1,0:T(8,128)S(1)}, f32[3,16,128]{2,1,0:T(8,128)S(1)}, u32[]{:S(2)}, u32[]{:S(2)}) collective-permute-start(f32[3,16,128]{2,1,0:T(8,128)S(1)} %pad_maximum_fusion), channel_id=1, source_target_pairs={{0,128},{32,160},{64,192},{96,224},{1,129},{33,161},{65,193},{97,2... | collective-permute-start | bytes 73736 | tf_op jit(solution)/shard_map/ppermute | solution.py:335
  34.6 8.8 %collective-permute-start.1 = (f32[3,16,128]{2,1,0:T(8,128)S(1)}, f32[3,16,128]{2,1,0:T(8,128)S(1)}, u32[]{:S(2)}, u32[]{:S(2)}) collective-permute-start(f32[3,16,128]{2,1,0:T(8,128)S(1)} %pad_maximum_fusion), channel_id=1, source_target_pairs={{0,256},{32,288},{64,320},{96,352},{1,257},{33,289},{65,321},{97,3... | collective-permute-start | bytes 73736 | tf_op jit(solution)/shard_map/ppermute | solution.py:335
  41.9 4.5 %collective-permute-start.2 = (f32[3,16,128]{2,1,0:T(8,128)S(1)}, f32[3,16,128]{2,1,0:T(8,128)S(1)}, u32[]{:S(2)}, u32[]{:S(2)}) collective-permute-start(f32[3,16,128]{2,1,0:T(8,128)S(1)} %pad_maximum_fusion), channel_id=1, source_target_pairs={{0,384},{32,416},{64,448},{96,480},{1,385},{33,417},{65,449},{97,4... | collective-permute-start | bytes 73736 | tf_op jit(solution)/shard_map/ppermute | solution.py:335
  78.5 1.9 %copy-start.1 = (f32[16,10,16,128]{3,2,1,0:T(8,128)}, f32[16,10,16,128]{3,2,1,0:T(8,128)S(1)}, u32[]{:S(2)}) copy-start(f32[16,10,16,128]{3,2,1,0:T(8,128)S(1)} %all_to_all.21.own) | copy-start | bytes 3932164
  78.5 8.0 %collective-permute-start.3 = (f32[16,10,16,128]{3,2,1,0:T(8,128)S(1)}, f32[16,10,16,128]{3,2,1,0:T(8,128)}, u32[]{:S(2)}, u32[]{:S(2)}) collective-permute-start(f32[16,10,16,128]{3,2,1,0:T(8,128)S(1)} %all_to_all.21.own), channel_id=1, source_target_pairs={{0,1},{1,0},{2,3},{3,2},{4,5},{5,4},{6,7},{7,6},{8,9},{9,8},{10,11... | collective-permute-start | bytes 3932168 | tf_op jit(solution)/shard_map/ppermute | solution.py:325
  80.4 38.8 %all-to-all-start.3 = ((f32[32,4,2,16,128]{4,3,2,1,0:T(8,128)}), f32[32,4,2,16,128]{4,3,2,1,0:T(8,128)S(1)}, u32[]{:S(2)}, u32[]{:S(2)}) async-start(f32[32,4,2,16,128]{4,3,2,1,0:T(8,128)} %broadcast_in_dim.6), calls=%async_computation.3 | async-start | bytes 4194304 | tf_op jit(solution)/shard_map/all_to_all | solution.py:322
  119.3 1.4 copy-start
Sparse Core Ops, SparseCore 0:
  43.3 70.2 all-gather.2

commit v5 on v4

--- a/solution.py
+++ b/solution.py
@@ -198,23 +198,37 @@
     out, raw_left, raw_top, left_rows, top_cols, e, v, o, d, w, sems,
 ):
     row, col = lax.axis_index("row"), lax.axis_index("col")
-    pairs = [(inv01, v.at[pl.ds(0, 2)]), (top.at[pl.ds(0, KP)], raw_top), (left, raw_left), (early, e), (over, o)]
+    pairs = [(inv01, v.at[pl.ds(0, 2)]), (top.at[pl.ds(0, KP)], raw_top), (early, e), (left, raw_left), (over, o)]
     pairs += [(inv23, v.at[pl.ds(2, 2)]), (diag, d), (kernel, w)]
     copies = _fetch(pairs, sems)
     offs = {(0, 1): e.at[2], (2, 3): o.at[4]}
     offs.update({at: o.at[i] for i, at in enumerate([(0, 2), (0, 3), (1, 2), (1, 3)])})
     thin = raw_left.shape[3] // 2
-    for copy in copies:
-        copy.wait()
-    for k in range(KP):
+
+    def step_top(k):
         head = _square(lambda half: raw_top[k, _columns(half, NB), :])
+        for j in range(k):
+            head = head - _tn(offs[j, k][...], top_cols[j])
+        top_cols[k] = _nn(v[k], head)
+
+    def step_left(k):
         parts = [_square(lambda half: raw_left[:, k, l, _columns(half, thin), :]) for l in range(2)]
         for j in range(k):
-            head = head - _tn(offs[j, k][...], top_cols[j])
             parts = [parts[l] - _nn(left_rows[j, pl.ds(NB * l, NB)], offs[j, k][...]) for l in range(2)]
-        top_cols[k] = _nn(v[k], head)
         for l in range(2):
             left_rows[k, pl.ds(NB * l, NB)] = _nt(parts[l], v[k])
+
+    for copy in copies[:3]:
+        copy.wait()
+    step_top(0)
+    step_top(1)
+    for copy in copies[3:]:
+        copy.wait()
+    step_left(0)
+    step_left(1)
+    for k in (2, 3):
+        step_top(k)
+        step_left(k)
 
     def store(l, block):
         for half in range(2):

time: 141 us -> 141 us (level)
  no operation moved by 1% of the time
where the time goes in v5:
time: 141 us; the launch traced here: 140 us
  Pallas kernels  45.5 us (32%)
  starting transfers between devices  33.3 us (24%)
  blocking collectives  30.2 us (21%)
  between operations  13.6 us (10%)
  waiting for transfers between devices  11.6 us (8%)
  local copies, waits for them, and re-layouts  6 us (4%)
    pallas_call x3, Pallas kernels, _call(): pl.pallas_call(kernel, out_shape=out_shape, in_specs=[ANYWHERE] * len(ope...  45.5 us
    all_to_all x2, blocking collectives, spread(): return lax.all_to_all(whole, axis, 0, 0, axis_index_groups=groups)  30.2 us
    ppermute x3, starting transfers between devices, on_device(): lax.ppermute(mine, 'row', [(r, r + d) for r in range(KP)])  15.7 us
    all_to_all x1, starting transfers between devices, on_device(): scattered = lax.all_to_all(cut, 'col', 0, 0)[:KP]  9.55 us
    all_to_all x1, waiting for transfers between devices, on_device(): scattered = lax.all_to_all(cut, 'col', 0, 0)[:KP]  8.33 us
    all_to_all x1, starting transfers between devices, spread(): return lax.all_to_all(whole, axis, 0, 0, axis_index_groups=groups)  6.08 us
    ppermute x3, waiting for transfers between devices, on_device(): lax.ppermute(mine, 'row', [(r, r + d) for r in range(KP)])  3.21 us
  transfers between devices with their start and end apart: 7, of which 3 were waited for; matrix products, arithmetic and copies ran while one was open for 2% of the time, Pallas kernels for 23%

profile of v5, /device:TPU:6, one launch (start us, length us, event | category | flops | bytes accessed | tf_op | source)
XLA Modules:
  0.0 140.3 jit_solution(589488595911210547)
XLA Ops:
  6.5 0.0 copy-start.2
  6.5 2.0 %copy_bitcast_fusion = f32[32,2,16,128]{3,2,1,0:T(8,128)} fusion(f32[2,32,16,128]{3,2,1,0:T(8,128)} %bitcast.57), kind=kLoop, calls=%fused_computation | loop fusion | bytes 1048576 | tf_op jit(solution)/shard_map/transpose | solution.py:341
  8.5 9.6 %all-to-all-start = ((f32[32,2,16,128]{3,2,1,0:T(8,128)}), f32[32,2,16,128]{3,2,1,0:T(8,128)S(1)}, u32[]{:S(2)}, u32[]{:S(2)}) async-start(f32[32,2,16,128]{3,2,1,0:T(8,128)} %copy_bitcast_fusion), calls=%async_computation | async-start | bytes 1048576 | tf_op jit(solution)/shard_map/all_to_all | solution.py:342
  18.1 0.0 all-gather.3.cloned.1.call-start
  18.1 0.0 copy-done.2
  18.1 0.9 slice.40
  19.1 8.3 %all-to-all-done = f32[32,2,16,128]{3,2,1,0:T(8,128)S(1)} async-done(((f32[32,2,16,128]{3,2,1,0:T(8,128)}), f32[32,2,16,128]{3,2,1,0:T(8,128)S(1)}, u32[]{:S(2)}, u32[]{:S(2)}) %all-to-all-start) | async-done | bytes 524320 | tf_op jit(solution)/shard_map/all_to_all | solution.py:342
  27.4 7.1 %collective-permute-start = (f32[3,16,128]{2,1,0:T(8,128)S(1)}, f32[3,16,128]{2,1,0:T(8,128)S(1)}, u32[]{:S(2)}, u32[]{:S(2)}) collective-permute-start(f32[3,16,128]{2,1,0:T(8,128)S(1)} %pad_maximum_fusion), channel_id=1, source_target_pairs={{0,128},{32,160},{64,192},{96,224},{1,129},{33,161},{65,193},{97,2... | collective-permute-start | bytes 73736 | tf_op jit(solution)/shard_map/ppermute | solution.py:349
  34.6 7.3 %collective-permute-start.1 = (f32[3,16,128]{2,1,0:T(8,128)S(1)}, f32[3,16,128]{2,1,0:T(8,128)S(1)}, u32[]{:S(2)}, u32[]{:S(2)}) collective-permute-start(f32[3,16,128]{2,1,0:T(8,128)S(1)} %pad_maximum_fusion), channel_id=1, source_target_pairs={{0,256},{32,288},{64,320},{96,352},{1,257},{33,289},{65,321},{97,3... | collective-permute-start | bytes 73736 | tf_op jit(solution)/shard_map/ppermute | solution.py:349
  41.9 1.3 collective-permute-start.2
  43.2 0.0 all-gather.3.cloned.1.call-update
  43.2 0.0 collective-permute-done
  43.2 0.2 collective-permute-done.1
  43.4 3.0 %collective-permute-done.2 = f32[3,16,128]{2,1,0:T(8,128)S(1)} collective-permute-done((f32[3,16,128]{2,1,0:T(8,128)S(1)}, f32[3,16,128]{2,1,0:T(8,128)S(1)}, u32[]{:S(2)}, u32[]{:S(2)}) %collective-permute-start.2) | collective-permute-done | bytes 24608 | tf_op jit(solution)/shard_map/ppermute | solution.py:349
  46.4 1.6 %broadcast_in_dim.6 = f32[32,4,2,16,128]{4,3,2,1,0:T(8,128)} broadcast(f32[4,2,16,128]{3,2,1,0:T(8,128)S(1)} %slice.53), dimensions={1,2,3,4} | broadcast | bytes 2162688 | tf_op jit(solution)/shard_map/broadcast_in_dim | solution.py:333
  48.0 8.7 %all_to_all.20 = f32[4,3,16,128]{3,2,1,0:T(8,128)S(1)} all-to-all(f32[4,3,16,128]{3,2,1,0:T(8,128)S(1)} %broadcast_in_dim.7), channel_id=1, replica_groups={{0,32,64,96},{128,160,192,224},{256,288,320,352},{384,416,448,480},{1,3..., dimensions={0} | all-to-all | bytes 196608 | tf_op jit(solution)/shard_map/all_to_all | solution.py:336
  56.9 0.1 broadcast_in_dim.8
  57.0 21.5 %all_to_all.21.own = f32[16,10,16,128]{3,2,1,0:T(8,128)S(1)} all-to-all(f32[16,10,16,128]{3,2,1,0:T(8,128)S(1)} %broadcast_in_dim.8), channel_id=1, replica_groups={{0,2,4,6,8,10,12,14,16,18,20,22,24,26,28,30},{1,3,5,7,9,11,13,15,17,19,..., dimensions={0} | all-to-all | bytes 2621440 | tf_op jit(solution)/shard_map/all_to_all | solution.py:336
  78.5 0.0 copy-start.1
  78.5 1.9 %collective-permute-start.3 = (f32[16,10,16,128]{3,2,1,0:T(8,128)S(1)}, f32[16,10,16,128]{3,2,1,0:T(8,128)}, u32[]{:S(2)}, u32[]{:S(2)}) collective-permute-start(f32[16,10,16,128]{3,2,1,0:T(8,128)S(1)} %all_to_all.21.own), channel_id=1, source_target_pairs={{0,1},{1,0},{2,3},{3,2},{4,5},{5,4},{6,7},{7,6},{8,9},{9,8},{10,11... | collective-permute-start | bytes 3932168 | tf_op jit(solution)/shard_map/ppermute | solution.py:339
  80.4 0.0 copy-done.1
  80.4 6.1 %all-to-all-start.3 = ((f32[32,4,2,16,128]{4,3,2,1,0:T(8,128)}), f32[32,4,2,16,128]{4,3,2,1,0:T(8,128)S(1)}, u32[]{:S(2)}, u32[]{:S(2)}) async-start(f32[32,4,2,16,128]{4,3,2,1,0:T(8,128)} %broadcast_in_dim.6), calls=%async_computation.3 | async-start | bytes 4194304 | tf_op jit(solution)/shard_map/all_to_all | solution.py:336
  86.5 0.0 collective-permute-done.3.other
  86.5 14.7 %early.1 = (f32[3,256,256]{2,1,0:T(8,128)}, f32[2,256,256]{2,1,0:T(8,128)}) custom-call(f32[16,10,16,128]{3,2,1,0:T(8,128)} %copy-done.1, f32[16,10,16,128]{3,2,1,0:T(8,128)} %collective-permute-done.3.other), custom_call_target="tpu_custom_call" | custom-call | flops 12000000000 | bytes 4000000 | tf_op jit(solution)/shard_map/early/pallas_call | solution.py:271
  101.3 18.0 %late.1 = (f32[5,256,256]{2,1,0:T(8,128)}, f32[2,256,256]{2,1,0:T(8,128)}, f32[2,256,256]{2,1,0:T(8,128)}) custom-call(f32[16,10,16,128]{3,2,1,0:T(8,128)} %copy-done.1, f32[16,10,16,128]{3,2,1,0:T(8,128)} %collective-permute-done.3.other, f32[3,256,256]{2,1,0:T(8,128)} %get-tuple-element.20.upper.early, f32[2,256,256]{2,1,0:T(8,128)} %get-tuple-element.21.inverse.inv01), custom_call_target="tpu_custom_call" | custom-call | flops 16000000000 | bytes 4000000 | tf_op jit(solution)/shard_map/late/pallas_call | solution.py:271
  119.3 0.0 all-to-all-done.3.left
  119.3 0.0 copy-start
  119.3 0.0 all-gather.3.cloned.1.call-done
  119.3 1.3 copy-done
  120.6 12.8 %finish.1 = f32[2,512,128]{2,1,0:T(8,128)} custom-call(f32[2,512,128]{2,1,0:T(8,128)} %bitcast.58, f32[32,4,2,16,128]{4,3,2,1,0:T(8,128)} %copy-done, f32[16,512,128]{2,1,0:T(8,128)} %bitcast.60, f32[3,256,256]{2,1,0:T(8,128)} %get-tuple-element.20.upper.early, f32[2,256,256]{2,1,0:T(8,128)} %get-tuple-element.21.inverse.inv01, ...), custom_call_target="tpu_custom_call" | custom-call | flops 10000000000 | bytes 4000000 | tf_op jit(solution)/shard_map/finish/pallas_call | solution.py:271
  (16 shorter events, 0.1 us)
Async XLA Ops:
  6.5 11.6 %copy-start.2 = (f32[2,256,1,256]{3,2,1,0:T(1,128)S(1)}, f32[2,256,1,256]{3,2,1,0:T(1,128)}, u32[]{:S(2)}) copy-start(f32[2,256,1,256]{3,2,1,0:T(1,128)} %param.1) | copy-start | bytes 1572868
  8.5 18.9 %all-to-all-start = ((f32[32,2,16,128]{3,2,1,0:T(8,128)}), f32[32,2,16,128]{3,2,1,0:T(8,128)S(1)}, u32[]{:S(2)}, u32[]{:S(2)}) async-start(f32[32,2,16,128]{3,2,1,0:T(8,128)} %copy_bitcast_fusion), calls=%async_computation | async-start | bytes 1048576 | tf_op jit(solution)/shard_map/all_to_all | solution.py:342
  18.1 101.2 %all-gather.3.cloned.1.call-start = ((), (), s32[]{:S(2)}) async-start(), calls=%async_computation.4 | async-start | bytes 4456448 | tf_op jit(solution)/shard_map/all_gather | solution.py:345
  27.4 15.8 %collective-permute-start = (f32[3,16,128]{2,1,0:T(8,128)S(1)}, f32[3,16,128]{2,1,0:T(8,128)S(1)}, u32[]{:S(2)}, u32[]{:S(2)}) collective-permute-start(f32[3,16,128]{2,1,0:T(8,128)S(1)} %pad_maximum_fusion), channel_id=1, source_target_pairs={{0,128},{32,160},{64,192},{96,224},{1,129},{33,161},{65,193},{97,2... | collective-permute-start | bytes 73736 | tf_op jit(solution)/shard_map/ppermute | solution.py:349
  34.6 8.8 %collective-permute-start.1 = (f32[3,16,128]{2,1,0:T(8,128)S(1)}, f32[3,16,128]{2,1,0:T(8,128)S(1)}, u32[]{:S(2)}, u32[]{:S(2)}) collective-permute-start(f32[3,16,128]{2,1,0:T(8,128)S(1)} %pad_maximum_fusion), channel_id=1, source_target_pairs={{0,256},{32,288},{64,320},{96,352},{1,257},{33,289},{65,321},{97,3... | collective-permute-start | bytes 73736 | tf_op jit(solution)/shard_map/ppermute | solution.py:349
  41.9 4.5 %collective-permute-start.2 = (f32[3,16,128]{2,1,0:T(8,128)S(1)}, f32[3,16,128]{2,1,0:T(8,128)S(1)}, u32[]{:S(2)}, u32[]{:S(2)}) collective-permute-start(f32[3,16,128]{2,1,0:T(8,128)S(1)} %pad_maximum_fusion), channel_id=1, source_target_pairs={{0,384},{32,416},{64,448},{96,480},{1,385},{33,417},{65,449},{97,4... | collective-permute-start | bytes 73736 | tf_op jit(solution)/shard_map/ppermute | solution.py:349
  78.5 1.9 %copy-start.1 = (f32[16,10,16,128]{3,2,1,0:T(8,128)}, f32[16,10,16,128]{3,2,1,0:T(8,128)S(1)}, u32[]{:S(2)}) copy-start(f32[16,10,16,128]{3,2,1,0:T(8,128)S(1)} %all_to_all.21.own) | copy-start | bytes 3932164
  78.5 8.0 %collective-permute-start.3 = (f32[16,10,16,128]{3,2,1,0:T(8,128)S(1)}, f32[16,10,16,128]{3,2,1,0:T(8,128)}, u32[]{:S(2)}, u32[]{:S(2)}) collective-permute-start(f32[16,10,16,128]{3,2,1,0:T(8,128)S(1)} %all_to_all.21.own), channel_id=1, source_target_pairs={{0,1},{1,0},{2,3},{3,2},{4,5},{5,4},{6,7},{7,6},{8,9},{9,8},{10,11... | collective-permute-start | bytes 3932168 | tf_op jit(solution)/shard_map/ppermute | solution.py:339
  80.4 38.8 %all-to-all-start.3 = ((f32[32,4,2,16,128]{4,3,2,1,0:T(8,128)}), f32[32,4,2,16,128]{4,3,2,1,0:T(8,128)S(1)}, u32[]{:S(2)}, u32[]{:S(2)}) async-start(f32[32,4,2,16,128]{4,3,2,1,0:T(8,128)} %broadcast_in_dim.6), calls=%async_computation.3 | async-start | bytes 4194304 | tf_op jit(solution)/shard_map/all_to_all | solution.py:336
  119.3 1.4 copy-start
Sparse Core Ops, SparseCore 0:
  43.3 70.2 all-gather.2
